TPU v7x, 128 devices: a whole 4x4x4 slice. The times are simulated.
128 devices in a mesh: row: 8 (over y_lo, z), col: 16 (over x, y_hi, core).
Axes of the slice: x: 4, y: 4 (y_hi: 2, y_lo: 2; y = y_hi * 2 + y_lo), z: 4, core: 2. Of those that a mesh axis runs over, the one named last changes fastest.
Arguments:
- amplitudes: float32 [2, 4096, 2048], P(None, 'row', 'col'), may hold values from -6 to 6
- integrals: float32 [2, 1024, 128, 128], P(None, 'col'), may hold values from -0.1875 to 0.1875
- tile_rows: int32 [2, 1024], replicated, may hold values from 0 to 15
- tile_reader: int32 [2, 1024, 1], replicated, may hold values from 0 to 15, as said below
- tile_column: int32 [2, 1024], replicated, may hold values from 0 to 15
Outputs:
- ladder: float32 [4096, 32768], P('row', 'col')
Inputs may be any that keep to these rules, and one draw needn't show every extreme that they name: `tile_reader`: rows of one panel fall in aligned blocks of 64, one block for the tiles held by one index of col. For each panel and reader column, exactly 64 held tiles name it, and their pairs (tile_rows, tile_column) are all different. Within a block no reader column is named more than 8 times, and in every panel every block names some reader column exactly 8 times.
All inputs are finite; a program needn't handle non-finite values.
Results may differ from a plain program's by a relative error of at most 0.0001.
Values sent between devices are 32-bit elements; how exact they have to be, the bound alone decides.
No kernel may reach another device: no remote copies, remote signals or barrier semaphores. Data moves between devices by JAX's collectives and lax.ppermute only.
A program may use at most 192 MiB of HBM per device.

v0:
```python
import jax
import jax.numpy as jnp
from jax import lax
from jax.sharding import PartitionSpec as P

TILE = 128
STEPS = 2
KT_DEV = 1
NT_DEV = 16
CAP = 8


def ranks_of(readers, col_count):
    onehot = (readers[..., None] == jnp.arange(col_count, dtype=jnp.int32)).astype(jnp.int32)
    before = jnp.cumsum(onehot, axis=-2) - onehot
    return jnp.sum(before * onehot, axis=-1)


def shards(amplitudes, integrals, tile_rows, tile_reader, tile_column):
    col_count = lax.axis_size("col")
    own_column = lax.axis_index("col")
    pair_rows = amplitudes.shape[1]
    held_count = integrals.shape[1]
    slot_count = col_count * CAP
    tile_total = col_count * KT_DEV
    readers = tile_reader[:, :, 0].reshape(STEPS, col_count, held_count)
    places = ranks_of(readers, col_count)
    own_readers = lax.dynamic_index_in_dim(readers, own_column, 1, keepdims=False)
    own_places = lax.dynamic_index_in_dim(places, own_column, 1, keepdims=False)
    slot_ids = own_readers * CAP + own_places
    packer = (
        slot_ids[:, None, :] == jnp.arange(slot_count, dtype=jnp.int32)[None, :, None]
    ).astype(jnp.float32)
    matches = (
        (readers == own_column)[:, :, None, :]
        & (places[:, :, None, :] == jnp.arange(CAP, dtype=jnp.int32)[None, None, :, None])
    ).astype(jnp.int32)
    slot_rows = jnp.sum(
        matches * tile_rows.reshape(STEPS, col_count, 1, held_count), axis=3
    ).reshape(STEPS, slot_count)
    slot_cols = jnp.sum(
        matches * tile_column.reshape(STEPS, col_count, 1, held_count), axis=3
    ).reshape(STEPS, slot_count)
    empty_out = jnp.zeros((pair_rows, NT_DEV * TILE), jnp.float32)
    ladder = empty_out
    for step_index in range(STEPS):
        outgoing = jnp.einsum(
            "sh,hkn->skn",
            packer[step_index],
            integrals[step_index],
            precision=lax.Precision.HIGHEST,
        )
        arrived = lax.all_to_all(
            outgoing.reshape(col_count, CAP, TILE, TILE),
            "col",
            split_axis=0,
            concat_axis=0,
            tiled=True,
        )
        arrived = arrived.reshape(slot_count, TILE, TILE)
        block = jnp.zeros((tile_total, TILE, NT_DEV, TILE), jnp.float32)
        block = block.at[slot_rows[step_index], :, slot_cols[step_index], :].add(arrived)
        block = block.reshape(tile_total * TILE, NT_DEV * TILE)
        ladder = ladder + jnp.dot(
            lax.all_gather(amplitudes[step_index], "col", axis=1, tiled=True),
            block,
            precision=lax.Precision.HIGHEST,
            preferred_element_type=jnp.float32,
        )
    return ladder


def solution(mesh):
    return jax.shard_map(
        shards,
        mesh=mesh,
        in_specs=(P(None, "row", "col"), P(None, "col", None, None), P(), P(), P()),
        out_specs=P("row", "col"),
        check_vma=False,
    )
```

profile of v0, /device:TPU:29, one launch (start us, length us, event | category | flops | bytes accessed | tf_op | source)
XLA Modules:
  0.0 507.5 jit_solution(10461883380164362155)
XLA Ops:
  6.5 0.7 reduce
  7.3 0.1 reshape_squeeze.3
  7.3 0.1 copy.41
  7.4 3.0 select_reduce_fusion
  10.4 0.2 add_reduce_fusion
  10.6 6.3 %fusion.24 = (f32[1,64,128,128]{3,2,1,0:T(8,128)}, f32[1,64,128,128]{3,2,1,0:T(8,128)S(1)}) fusion(f32[2,64,128,128]{3,2,1,0:T(8,128)} %param.6), kind=kLoop, calls=%fused_computation.44 | loop fusion | bytes 16777216 | tf_op jit(solution)/shard_map/slice | solution.py:50
  17.0 9.3 %fusion.6 = f32[16,8,128,128]{3,1,2,0:T(8,128)} fusion(f32[1,64,128,128]{3,2,1,0:T(8,128)S(1)} %get-tuple-element.8, pred[2,128,64]{2,1,0:T(32,128)(4,1)S(1)} %iota_compare_fusion.2), kind=kOutput, calls=%fused_computation.9 | convolution fusion | flops 1610612736 | bytes 12599296 | tf_op jit(solution)/shard_map/sh,hkn->skn/dot_general | solution.py:47
  26.3 7.7 %all-to-all-start.1 = ((f32[16,8,128,128]{3,1,2,0:T(8,128)}), f32[16,8,128,128]{3,1,2,0:T(8,128)}, u32[]{:S(2)}, u32[]{:S(2)}) async-start(f32[16,8,128,128]{3,1,2,0:T(8,128)} %fusion.6), calls=%async_computation.1 | async-start | bytes 16777216 | tf_op jit(solution)/shard_map/all_to_all | solution.py:53
  34.0 0.8 fusion.25
  34.9 13.4 %fusion.7 = f32[16,8,128,128]{3,1,2,0:T(8,128)} fusion(f32[1,64,128,128]{3,2,1,0:T(8,128)} %get-tuple-element.7, pred[2,128,64]{2,1,0:T(32,128)(4,1)S(1)} %iota_compare_fusion.2), kind=kOutput, calls=%fused_computation.11 | convolution fusion | flops 1610612736 | bytes 12599296 | tf_op jit(solution)/shard_map/sh,hkn->skn/dot_general | solution.py:47
  48.3 117.1 %all-to-all-done.1 = f32[16,8,128,128]{3,1,2,0:T(8,128)} async-done(((f32[16,8,128,128]{3,1,2,0:T(8,128)}), f32[16,8,128,128]{3,1,2,0:T(8,128)}, u32[]{:S(2)}, u32[]{:S(2)}) %all-to-all-start.1) | async-done | bytes 8388640 | tf_op jit(solution)/shard_map/all_to_all | solution.py:53
  165.3 7.1 %all-to-all-start = ((f32[16,8,128,128]{3,1,2,0:T(8,128)}), f32[16,8,128,128]{3,1,2,0:T(8,128)}, u32[]{:S(2)}, u32[]{:S(2)}) async-start(f32[16,8,128,128]{3,1,2,0:T(8,128)} %fusion.7), calls=%async_computation | async-start | bytes 16777216 | tf_op jit(solution)/shard_map/all_to_all | solution.py:53
  172.4 0.3 all-gather.5.cloned.1.call-start
  172.7 0.4 all-gather.5.cloned.1.call-update
  173.2 0.1 mul.31
  173.4 1.2 select_reduce_fusion.2
  174.6 0.1 squeeze.33
  174.7 0.1 squeeze.34
  174.7 0.1 squeeze.29
  174.8 0.1 squeeze.30
  175.0 8.1 %copy.48 = f32[16,8,128,128]{3,2,1,0:T(8,128)} copy(f32[16,8,128,128]{3,1,2,0:T(8,128)} %all-to-all-done.1) | data formatting | bytes 16777216 | tf_op jit(solution)/shard_map/all_to_all | solution.py:53
  183.0 8.0 %broadcast.78.clone = f32[16,128,16,128]{3,1,2,0:T(8,128)} broadcast(f32[]{:T(128)} %constant.20.clone.1), dimensions={} | broadcast | bytes 16777220 | tf_op jit(solution)/shard_map/broadcast.5
  191.0 26.9 %scatter_fusion.1 = f32[16,128,16,128]{3,1,2,0:T(8,128)} fusion(f32[16,128,16,128]{3,1,2,0:T(8,128)} %broadcast.78.clone, s32[128]{0:T(128)S(1)} %fusion.23, f32[128,128,128]{2,1,0:T(8,128)} %bitcast.51), kind=kCustom, calls=%fused_computation.1 | custom fusion | flops 2097152 | bytes 25166848 | tf_op jit(solution)/shard_map/scatter-add | solution.py:62
  217.9 17.7 %copy.49 = f32[16,128,16,128]{3,2,1,0:T(8,128)} copy(f32[16,128,16,128]{3,1,2,0:T(8,128)} %scatter_fusion.1) | data formatting | bytes 33554432 | tf_op jit(solution)/shard_map/scatter-add | solution.py:62
  235.6 68.1 %all-to-all-done = f32[16,8,128,128]{3,1,2,0:T(8,128)} async-done(((f32[16,8,128,128]{3,1,2,0:T(8,128)}), f32[16,8,128,128]{3,1,2,0:T(8,128)}, u32[]{:S(2)}, u32[]{:S(2)}) %all-to-all-start) | async-done | bytes 8388640 | tf_op jit(solution)/shard_map/all_to_all | solution.py:53
  303.7 8.1 %copy.45 = f32[16,8,128,128]{3,2,1,0:T(8,128)} copy(f32[16,8,128,128]{3,1,2,0:T(8,128)} %all-to-all-done) | data formatting | bytes 16777216 | tf_op jit(solution)/shard_map/all_to_all | solution.py:53
  311.7 7.8 %broadcast.78.clone.1 = f32[16,128,16,128]{3,1,2,0:T(8,128)} broadcast(f32[]{:T(128)} %constant.20.clone.1), dimensions={} | broadcast | bytes 16777220 | tf_op jit(solution)/shard_map/broadcast.5
  319.6 26.5 %scatter_fusion = f32[16,128,16,128]{3,1,2,0:T(8,128)} fusion(f32[16,128,16,128]{3,1,2,0:T(8,128)} %broadcast.78.clone.1, s32[128]{0:T(128)S(1)} %fusion.22, f32[128,128,128]{2,1,0:T(8,128)} %bitcast.50), kind=kCustom, calls=%fused_computation | custom fusion | flops 2097152 | bytes 25166848 | tf_op jit(solution)/shard_map/scatter-add | solution.py:62
  346.1 17.7 %copy.46 = f32[16,128,16,128]{3,2,1,0:T(8,128)} copy(f32[16,128,16,128]{3,1,2,0:T(8,128)} %scatter_fusion) | data formatting | bytes 33554432 | tf_op jit(solution)/shard_map/scatter-add | solution.py:62
  363.8 68.6 %fusion = f32[2048,512]{1,0:T(8,128)} fusion(f32[256,8,16,128]{3,2,1,0:T(8,128)} %bitcast.52, f32[1,512,2048]{2,1,0:T(8,128)} %all-gather.7.cloned.1.call-done), kind=kOutput, calls=%fused_computation.2 | convolution fusion | flops 25769803776 | bytes 25165824 | tf_op jit(solution)/shard_map/dot_general | solution.py:64
  432.4 62.5 %add_bitcast_fusion = f32[512,2048]{0,1:T(8,128)} fusion(f32[2048,512]{1,0:T(8,128)} %fusion, f32[1,512,2048]{2,1,0:T(8,128)} %all-gather.5.cloned.1.call-done, f32[256,8,16,128]{3,2,1,0:T(8,128)} %bitcast.53), kind=kOutput, calls=%fused_computation.14 | convolution fusion | flops 25770852352 | bytes 29360128 | tf_op jit(solution)/shard_map/dot_general | solution.py:64
  494.9 5.3 %copy.50 = f32[512,2048]{1,0:T(8,128)} copy(f32[512,2048]{0,1:T(8,128)} %add_bitcast_fusion) | data formatting | bytes 8388608 | tf_op jit(solution)/shard_map/add | solution.py:64
  (17 shorter events, 0.3 us)
Async XLA Ops:
  26.3 7.7 %copy-start = (f32[2,512,128]{2,1,0:T(8,128)S(1)}, f32[2,512,128]{2,1,0:T(8,128)}, u32[]{:S(2)}) copy-start(f32[2,512,128]{2,1,0:T(8,128)} %param.5) | copy-start | bytes 1572868
  26.3 139.0 %all-to-all-start.1 = ((f32[16,8,128,128]{3,1,2,0:T(8,128)}), f32[16,8,128,128]{3,1,2,0:T(8,128)}, u32[]{:S(2)}, u32[]{:S(2)}) async-start(f32[16,8,128,128]{3,1,2,0:T(8,128)} %fusion.6), calls=%async_computation.1 | async-start | bytes 16777216 | tf_op jit(solution)/shard_map/all_to_all | solution.py:53
  33.9 329.8 %all-gather.7.cloned.1.call-start = ((), (), s32[]{:S(2)}) async-start(), calls=%async_computation.3 | async-start | bytes 4456448 | tf_op jit(solution)/shard_map/all_gather | solution.py:65
  48.3 125.0 %copy-start.1 = (s32[2,1024]{1,0:T(2,128)S(1)}, s32[2,1024]{1,0:T(2,128)}, u32[]{:S(2)}) copy-start(s32[2,1024]{1,0:T(2,128)} %param.7) | copy-start | bytes 24580
  48.3 125.0 %copy-start.2 = (s32[2,1024]{1,0:T(2,128)S(1)}, s32[2,1024]{1,0:T(2,128)}, u32[]{:S(2)}) copy-start(s32[2,1024]{1,0:T(2,128)} %param.9) | copy-start | bytes 24580
  165.3 138.3 %all-to-all-start = ((f32[16,8,128,128]{3,1,2,0:T(8,128)}), f32[16,8,128,128]{3,1,2,0:T(8,128)}, u32[]{:S(2)}, u32[]{:S(2)}) async-start(f32[16,8,128,128]{3,1,2,0:T(8,128)} %fusion.7), calls=%async_computation | async-start | bytes 16777216 | tf_op jit(solution)/shard_map/all_to_all | solution.py:53
  172.4 260.0 %all-gather.5.cloned.1.call-start = ((), (), s32[]{:S(2)}) async-start(), calls=%async_computation.2 | async-start | bytes 4456448 | tf_op jit(solution)/shard_map/all_gather | solution.py:65
Sparse Core Ops, SparseCore 0:
  37.0 124.7 all-gather.6
  175.5 124.6 all-gather.4
where the time goes:
time: 516 us; the launch traced here: 507 us
  waiting for transfers between devices  186 us (36%)
  matrix products  154 us (30%)
  local copies, waits for them, and re-layouts  80.6 us (16%)
  other arithmetic  58.5 us (11%)
  starting transfers between devices  15.1 us (3%)
  between operations  13.9 us (3%)
    all_to_all x2, waiting for transfers between devices, shards(): lax.all_to_all(outgoing.reshape(col_count, CAP, TILE, TILE), 'col', split...  185 us
    dot_general x2, matrix products, shards(): jnp.dot(lax.all_gather(amplitudes[step_index], 'col', axis=1, tiled=True)...  131 us
    scatter-add x2, other arithmetic, shards(): block.at[slot_rows[step_index], :, slot_cols[step_index], :].add(arrived)  53.4 us
    scatter-add x2, local copies, waits for them, and re-layouts, shards(): block.at[slot_rows[step_index], :, slot_cols[step_index], :].add(arrived)  35.4 us
    dot_general x2, matrix products, shards(): jnp.einsum('sh,hkn->skn', packer[step_index], integrals[step_index], prec...  22.7 us
    all_to_all x2, local copies, waits for them, and re-layouts, shards(): lax.all_to_all(outgoing.reshape(col_count, CAP, TILE, TILE), 'col', split...  16.1 us
    another operation x2, local copies, waits for them, and re-layouts  15.8 us
    all_to_all x2, starting transfers between devices, shards(): lax.all_to_all(outgoing.reshape(col_count, CAP, TILE, TILE), 'col', split...  14.7 us
  transfers between devices with their start and end apart: 4, of which 2 were waited for; matrix products, arithmetic and copies ran while one was open for 40% of the time, Pallas kernels for 0%

commit v1 on v0

v1 whole, which is shorter than its diff:
```python
import functools

import jax
import jax.numpy as jnp
from jax import lax
from jax.experimental import pallas as pl
from jax.experimental.pallas import tpu as pltpu
from jax.sharding import PartitionSpec as P

TILE = 128
STEPS = 2
NT_DEV = 16
N_COL = 16
N_ROW = 8
Z = 4
HOLD = 64
CHUNK = HOLD // N_ROW
LANES = 128
VMEM_LIMIT = 56 * 1024 * 1024


def route_kernel(reader_ref, row_ref, column_ref, tiles_ref, meta_ref, *rest):
    out_ref, meta_smem, meta_sem, sems = rest
    me_row = lax.axis_index("row")
    me_col = lax.axis_index("col")
    groups = reader_ref.shape[1]
    lane = lax.broadcasted_iota(jnp.int32, (1, LANES), 1)
    upto = (
        lax.broadcasted_iota(jnp.int32, (LANES, LANES), 0)
        <= lax.broadcasted_iota(jnp.int32, (LANES, LANES), 1)
    ).astype(jnp.bfloat16)
    names = lax.broadcasted_iota(jnp.int32, (N_COL, LANES), 0)
    numbers = lax.broadcasted_iota(jnp.int32, (HOLD, LANES), 0)
    ones = jnp.ones((8, LANES), jnp.bfloat16)

    def to_lanes(sums):
        return lax.dot_general(
            ones, sums.astype(jnp.bfloat16), (((1,), (1,)), ((), ())), preferred_element_type=jnp.float32
        )

    for s in range(STEPS):
        readers = reader_ref[s]
        named = [(readers[g : g + 1] == names) for g in range(groups)]
        onehot = jnp.concatenate([n.astype(jnp.bfloat16) for n in named], axis=0)
        within = jnp.dot(onehot, upto, preferred_element_type=jnp.float32)
        before = jnp.zeros((N_COL, 1), jnp.float32)
        send = jnp.zeros((N_COL, LANES), jnp.float32)
        code = jnp.zeros((HOLD, LANES), jnp.float32)
        holder = jnp.zeros((HOLD, LANES), jnp.float32)
        for g in range(groups):
            count = within[g * N_COL : (g + 1) * N_COL]
            number = (count + before - 1.0).astype(jnp.int32)
            before = before + count[:, LANES - 1 :]
            held = lane + g * LANES
            sent = named[g] & (held // HOLD == me_col) & (number % N_ROW == me_row)
            send = send + jnp.where(sent, (held % HOLD).astype(jnp.float32), 0.0)
            place = jnp.sum(jnp.where(named[g], number, 0), axis=0, keepdims=True)
            mine = (place == numbers) & (readers[g : g + 1] == me_col)
            tile_code = row_ref[s, g : g + 1] * NT_DEV + column_ref[s, g : g + 1]
            code = code + jnp.where(mine, tile_code.astype(jnp.float32), 0.0)
            holder = holder + jnp.where(mine, (held // HOLD).astype(jnp.float32), 0.0)
        parts = [to_lanes(code)[:1], to_lanes(holder)[:1], to_lanes(send)[:1]]
        for at, part in enumerate(parts):
            meta_ref[s * 8 + at : s * 8 + at + 1, : part.shape[1]] = part.astype(jnp.int32)
    copy = pltpu.make_async_copy(meta_ref, meta_smem, meta_sem)
    copy.start()
    copy.wait()
    copies = []
    for s in range(STEPS):
        for r in range(N_COL):
            tile = meta_smem[s * 8 + 2, r]
            copies.append(
                pltpu.make_async_copy(tiles_ref.at[s, tile], out_ref.at[r, s], sems.at[len(copies)])
            )
            copies[-1].start()
    for copy in copies:
        copy.wait()


def route(readers, rows, columns, tiles):
    vmem = pl.BlockSpec(memory_space=pltpu.VMEM)
    return pl.pallas_call(
        route_kernel,
        out_shape=(
            jax.ShapeDtypeStruct((8 * STEPS, LANES), jnp.int32),
            jax.ShapeDtypeStruct((N_COL, STEPS, TILE, TILE), jnp.float32),
        ),
        in_specs=[vmem, vmem, vmem, pl.BlockSpec(memory_space=pltpu.HBM)],
        out_specs=(vmem, vmem),
        scratch_shapes=[
            pltpu.SMEM((8 * STEPS, LANES), jnp.int32),
            pltpu.SemaphoreType.DMA,
            pltpu.SemaphoreType.DMA((STEPS * N_COL,)),
        ],
        name="route",
    )(readers, rows, columns, tiles)


def compact_kernel(passed, meta_ref, arrived_ref, *rest):
    out_ref, sems = rest[-2 - passed], rest[-1]
    me_row = lax.axis_index("row")
    copies = []
    for s in range(STEPS):
        for j in range(CHUNK):
            holder = meta_ref[s * 8 + 1, j * N_ROW + me_row]
            at = len(copies)
            copies.append(pltpu.make_async_copy(arrived_ref.at[holder, s], out_ref.at[at], sems.at[at]))
            copies[-1].start()
    for copy in copies:
        copy.wait()


def compact(meta, arrived, passed):
    tiles = STEPS * CHUNK
    hbm = pl.BlockSpec(memory_space=pltpu.HBM)
    return pl.pallas_call(
        functools.partial(compact_kernel, len(passed)),
        out_shape=[jax.ShapeDtypeStruct((tiles, TILE, TILE), jnp.float32)]
        + [jax.ShapeDtypeStruct(p.shape, p.dtype) for p in passed],
        grid_spec=pltpu.PrefetchScalarGridSpec(
            num_scalar_prefetch=1,
            grid=(1,),
            in_specs=[hbm] * (1 + len(passed)),
            out_specs=[pl.BlockSpec((tiles, TILE, TILE), lambda n, meta: (0, 0, 0))] + [hbm] * len(passed),
            scratch_shapes=[pltpu.SemaphoreType.DMA((tiles,))],
        ),
        input_output_aliases={2 + n: 1 + n for n in range(len(passed))},
        name="compact",
    )(meta, arrived, *passed)


def regroup_kernel(plan, passed, *refs):
    outs, sems = refs[-1 - passed - len(plan) : -1 - passed], refs[-1]
    copies = []
    for out, parts in zip(outs, plan):
        begin = 0
        for source, first, size in parts:
            copies.append(
                pltpu.make_async_copy(
                    refs[source].at[pl.ds(first, size)], out.at[pl.ds(begin, size)], sems.at[len(copies)]
                )
            )
            copies[-1].start()
            begin += size
    for copy in copies:
        copy.wait()


def regroup(chunks, plan, passed=(), earlier=()):
    any_space, hbm = pl.BlockSpec(memory_space=pl.ANY), pl.BlockSpec(memory_space=pltpu.HBM)
    shapes = [(sum(size for _, _, size in parts),) + chunks[0].shape[1:] for parts in plan]
    before = len(chunks) + len(earlier)
    return pl.pallas_call(
        functools.partial(regroup_kernel, plan, len(passed)),
        out_shape=[jax.ShapeDtypeStruct(shape, jnp.float32) for shape in shapes]
        + [jax.ShapeDtypeStruct(p.shape, p.dtype) for p in passed],
        in_specs=[any_space] * before + [hbm] * len(passed),
        out_specs=[pl.BlockSpec(memory_space=pltpu.VMEM)] * len(plan) + [hbm] * len(passed),
        scratch_shapes=[pltpu.SemaphoreType.DMA((sum(len(parts) for parts in plan),))],
        input_output_aliases={before + n: len(plan) + n for n in range(len(passed))},
        compiler_params=pltpu.CompilerParams(vmem_limit_bytes=VMEM_LIMIT),
        name="regroup",
    )(*chunks, *earlier, *passed)


def split_kernel(*refs):
    out_ref = refs[-1]
    for at, ref in enumerate(refs[:-1]):
        value = ref[0]
        high = value.astype(jnp.bfloat16)
        out_ref[at // 8, at // 4 % 2, at % 4, 0, :, :TILE] = high
        out_ref[at // 8, at // 4 % 2, at % 4, 0, :, TILE:] = (value - high.astype(jnp.float32)).astype(jnp.bfloat16)


def split_amplitudes(pieces):
    panels, rows = pieces[0].shape[:2]
    return pl.pallas_call(
        split_kernel,
        out_shape=jax.ShapeDtypeStruct((2, 2, 4, panels, rows, 2 * TILE), jnp.bfloat16),
        grid=(panels, 2),
        in_specs=[pl.BlockSpec((1, rows // 2, TILE), lambda s, n: (s, n, 0))] * 16,
        out_specs=pl.BlockSpec((2, 2, 4, 1, rows // 2, 2 * TILE), lambda s, n: (0, 0, 0, s, n, 0)),
        compiler_params=pltpu.CompilerParams(vmem_limit_bytes=VMEM_LIMIT),
        cost_estimate=pl.CostEstimate(flops=2**20, bytes_accessed=24 * 2**20, transcendentals=0),
        name="split_amplitudes",
    )(*pieces)


def product_kernel(places, has_start, meta_ref, *rest):
    chunk_refs = rest[: len(places)]
    amp_ref = rest[len(places)]
    out_ref = rest[-1]
    me_row = lax.axis_index("row")
    me_col = lax.axis_index("col")
    block = out_ref.shape[0] // 2
    if has_start:
        out_ref[...] = rest[len(places) + 1][...]
    else:
        out_ref[...] = jnp.zeros_like(out_ref)
    for ref, runs in zip(chunk_refs, places):
        at = 0
        for dy, dz, first, count in runs:
            source = ((me_row // Z) ^ dy) * Z + (me_row + dz) % Z

            def step(m, ref=ref, source=source, at=at, first=first):
                number = first + m
                s = number // CHUNK
                code = meta_ref[s * 8, (number % CHUNK) * N_ROW + source]
                column = code // NT_DEV
                away = (column // 4 + 4 - me_col // 4) % 4
                tile = ref[at + m]
                high = tile.astype(jnp.bfloat16)
                low = (tile - high.astype(jnp.float32)).astype(jnp.bfloat16)
                wide = jnp.concatenate([high, low], axis=1)
                wide = jnp.concatenate([wide, wide], axis=0)
                columns = pl.ds(pl.multiple_of((code % NT_DEV) * TILE, TILE), TILE)
                for begin in range(0, out_ref.shape[0], block):
                    rows = pl.ds(begin, block)
                    both = jnp.dot(
                        amp_ref[((column ^ me_col) // 2) % 2, (column ^ me_col) % 2, away, s, rows],
                        wide,
                        preferred_element_type=jnp.float32,
                    )
                    out_ref[rows, columns] += both[:, :TILE] + both[:, TILE:]

            pl.loop(0, count, unroll=min(count, 4))(step)
            at += count


def product(meta, chunks, places, amps, start=None):
    vmem = pl.BlockSpec(memory_space=pltpu.VMEM)
    rows = amps.shape[4]
    operands = list(chunks) + [amps] + ([] if start is None else [start])
    tiles = sum(c.shape[0] for c in chunks)
    return pl.pallas_call(
        functools.partial(product_kernel, places, start is not None),
        out_shape=jax.ShapeDtypeStruct((rows, NT_DEV * TILE), jnp.float32),
        in_specs=[pl.BlockSpec(memory_space=pltpu.SMEM)] + [vmem] * len(operands),
        out_specs=vmem,
        compiler_params=pltpu.CompilerParams(vmem_limit_bytes=VMEM_LIMIT),
        cost_estimate=pl.CostEstimate(
            flops=6 * tiles * rows * 4 * TILE * TILE, bytes_accessed=8 * 2**20, transcendentals=0
        ),
        name="product",
    )(meta, *operands)


def along_z(value, step):
    pairs = [(i, (i // Z) * Z + (i % Z + step) % Z) for i in range(N_ROW)]
    return lax.ppermute(value, "row", pairs)


def across_y(value):
    return lax.ppermute(value, "row", [(i, i ^ Z) for i in range(N_ROW)])


def along_x(value, step):
    pairs = [(c, ((c // 4 + step) % 4) * 4 + c % 4) for c in range(N_COL)]
    return lax.ppermute(value, "col", pairs)


def flip(value, bit):
    return lax.ppermute(value, "col", [(c, c ^ bit) for c in range(N_COL)])


def shards(amplitudes, integrals, tile_rows, tile_reader, tile_column):
    held = (STEPS, tile_rows.shape[1] // LANES, LANES)
    meta, sent = route(
        tile_reader.reshape(held), tile_rows.reshape(held), tile_column.reshape(held), integrals
    )
    side, amp_right, amp_left = flip(amplitudes, 2), along_x(amplitudes, -1), along_x(amplitudes, 1)
    arrived = lax.all_to_all(sent, "col", split_axis=0, concat_axis=0, tiled=True)
    own, side, amp_right, amp_left = compact(meta, arrived, (side, amp_right, amp_left))

    left, right, other = along_z(own, 1), along_z(own, -1), across_y(own)
    side_around = [along_x(side, step) for step in (-1, 2, 1)]
    amp_far = along_x(amp_left, 1)
    flipped = [flip(p, 1) for p in (amplitudes, amp_right, amp_left, side)]

    up, down, across, amp_far, *side_around = regroup(
        [left, right, other],
        [[(0, 0, 8), (2, 0, 8)], [(1, 8, 8), (2, 8, 8)], [(0, 8, 8), (1, 0, 8)]],
        [amp_far] + side_around,
        flipped,
    )
    up, down, across = along_z(up, 1), along_z(down, -1), across_y(across)
    flipped = flipped[:2] + [flip(amp_far, 1)] + flipped[2:] + [flip(p, 1) for p in side_around]
    amps = split_amplitudes([amplitudes, amp_right, amp_far, amp_left] + flipped[:4] + [side] + side_around + flipped[4:])
    places = [[(dy, dz, 0, 16)] for dy, dz in ((0, 0), (0, 3), (0, 1), (1, 0))]
    ladder = product(meta, [own, left, right, other], places, amps)

    far_up, far_down, far_across = regroup(
        [up, down], [[(0, 8, 5)], [(1, 11, 5)], [(0, 5, 3), (1, 0, 3)]], (), [ladder]
    )
    far_up, far_down, far_across = along_z(far_up, 1), along_z(far_down, -1), across_y(far_across)
    places = [
        [(0, 2, 0, 8), (1, 3, 0, 8)],
        [(0, 2, 8, 8), (1, 1, 8, 8)],
        [(1, 3, 8, 8), (1, 1, 0, 8)],
    ]
    ladder = product(meta, [up, down, across], places, amps, ladder)
    places = [[(1, 2, 0, 5)], [(1, 2, 11, 5)], [(1, 2, 5, 6)]]
    return product(meta, [far_up, far_down, far_across], places, amps, ladder)


def solution(mesh):
    return jax.shard_map(
        shards,
        mesh=mesh,
        in_specs=(P(None, "row", "col"), P(None, "col", None, None), P(), P(), P()),
        out_specs=P("row", "col"),
        check_vma=False,
    )
```

time: 516 us -> 181 us (0.35)
  the two profiles are of different devices: /device:TPU:29 before, /device:TPU:6 now
where the time goes in v1:
time: 181 us; the launch traced here: 178 us
  waiting for transfers between devices  61.2 us (34%)
  Pallas kernels  58.4 us (32%)
  starting transfers between devices  46.1 us (25%)
  local copies, waits for them, and re-layouts  12.2 us (7%)
    ppermute x6, waiting for transfers between devices, along_x(): return lax.ppermute(value, 'col', pairs)  61.2 us
    pallas_call x3, Pallas kernels, product(): pl.pallas_call(functools.partial(product_kernel, places, start is not Non...  36.8 us
    ppermute x6, starting transfers between devices, along_x(): return lax.ppermute(value, 'col', pairs)  18.3 us
    ppermute x6, starting transfers between devices, along_z(): return lax.ppermute(value, 'row', pairs)  12.5 us
    unnamed x48, local copies, waits for them, and re-layouts  10.8 us
    all_to_all x1, starting transfers between devices, shards(): lax.all_to_all(sent, 'col', split_axis=0, concat_axis=0, tiled=True)  7.49 us
    pallas_call x1, Pallas kernels, split_amplitudes(): pl.pallas_call(split_kernel, out_shape=jax.ShapeDtypeStruct((2, 2, 4, pan...  7.37 us
    pallas_call x2, Pallas kernels, regroup(): pl.pallas_call(functools.partial(regroup_kernel, plan, len(passed)), out_...  5.74 us
  transfers between devices with their start and end apart: 25, of which 4 were waited for; matrix products, arithmetic and copies ran while one was open for 0% of the time, Pallas kernels for 23%

profile of v1, /device:TPU:6, one launch (start us, length us, event | category | flops | bytes accessed | tf_op | source)
XLA Modules:
  0.0 178.1 jit_solution(2517202477769320206)
XLA Ops:
  0.0 1.3 copy_bitcast_fusion
  1.3 5.3 %route.1 = (s32[16,128]{1,0:T(8,128)}, f32[16,2,128,128]{3,2,1,0:T(8,128)}) custom-call(s32[2,8,128]{2,1,0:T(8,128)} %bitcast.7, s32[2,8,128]{2,1,0:T(8,128)} %get-tuple-element.38.row_ref, s32[2,8,128]{2,1,0:T(8,128)} %get-tuple-element.37.column_ref, f32[2,64,128,128]{3,2,1,0:T(8,128)} %tiles_ref.1), custom_call_target="tpu_custom_call" | custom-call | tf_op jit(solution)/shard_map/route/pallas_call | solution.py:82
  6.6 7.5 %all-to-all-start = ((f32[16,2,128,128]{3,2,1,0:T(8,128)}), f32[16,2,128,128]{3,2,1,0:T(8,128)S(1)}, u32[]{:S(2)}, u32[]{:S(2)}) async-start(f32[16,2,128,128]{3,2,1,0:T(8,128)} %get-tuple-element.22), calls=%async_computation | async-start | bytes 4194304 | tf_op jit(solution)/shard_map/all_to_all | solution.py:272
  14.3 1.9 %collective-permute-start.1 = (f32[2,512,128]{2,1,0:T(8,128)}, f32[2,512,128]{2,1,0:T(8,128)S(1)}, u32[]{:S(2)}, u32[]{:S(2)}) collective-permute-start(f32[2,512,128]{2,1,0:T(8,128)} %refs_0_.1), channel_id=1, source_target_pairs={{0,12},{1,13},{2,14},{3,15},{4,0},{5,1},{6,2},{7,3},{8,4},{9,5},{1... | collective-permute-start | bytes 1572872 | tf_op jit(solution)/shard_map/ppermute | solution.py:259
  16.1 3.0 %collective-permute-start = (f32[2,512,128]{2,1,0:T(8,128)}, f32[2,512,128]{2,1,0:T(8,128)}, u32[]{:S(2)}, u32[]{:S(2)}) collective-permute-start(f32[2,512,128]{2,1,0:T(8,128)} %refs_0_.1), channel_id=1, source_target_pairs={{0,2},{1,3},{2,0},{3,1},{4,6},{5,7},{6,4},{7,5},{8,10},{9,11},{10,... | collective-permute-start | bytes 1572872 | tf_op jit(solution)/shard_map/ppermute | solution.py:263
  19.1 33.3 %collective-permute-done.2.rest_2_ = f32[2,512,128]{2,1,0:T(8,128)S(1)} collective-permute-done((f32[2,512,128]{2,1,0:T(8,128)}, f32[2,512,128]{2,1,0:T(8,128)S(1)}, u32[]{:S(2)}, u32[]{:S(2)}) %collective-permute-start.2) | collective-permute-done | bytes 524320 | tf_op jit(solution)/shard_map/ppermute | solution.py:259
  52.4 0.8 copy-done.10
  53.4 1.2 copy-done
  54.6 3.1 %compact.1 = (f32[16,128,128]{2,1,0:T(8,128)}, f32[2,512,128]{2,1,0:T(8,128)}, f32[2,512,128]{2,1,0:T(8,128)}, f32[2,512,128]{2,1,0:T(8,128)}) custom-call(s32[16,128]{1,0:T(8,128)} %get-tuple-element.21.meta_ref, f32[16,2,128,128]{3,2,1,0:T(8,128)} %copy-done, ...), custom_call_target="tpu_custom_call", output_to_operand_aliasing={{1}: (2, {}), {2}: (3, {}), {3}: (4, {})} | custom-call | tf_op jit(solution)/shard_map/compact/pallas_call | solution.py:116
  58.9 3.2 %collective-permute-start.12 = (f32[2,512,128]{2,1,0:T(8,128)}, f32[2,512,128]{2,1,0:T(8,128)S(1)}, u32[]{:S(2)}, u32[]{:S(2)}) collective-permute-start(f32[2,512,128]{2,1,0:T(8,128)} %get-tuple-element.26.refs_8_), channel_id=1, source_target_pairs={{0,8},{1,9},{2,10},{3,11},{4,12},{5,13},{6,14},{7,15},{8,0},{9,1},... | collective-permute-start | bytes 1572872 | tf_op jit(solution)/shard_map/ppermute | solution.py:259
  62.1 1.3 collective-permute-start.5
  63.4 9.4 %collective-permute-done.10.refs_7_ = f32[2,512,128]{2,1,0:T(8,128)S(1)} collective-permute-done((f32[2,512,128]{2,1,0:T(8,128)}, f32[2,512,128]{2,1,0:T(8,128)S(1)}, u32[]{:S(2)}, u32[]{:S(2)}) %collective-permute-start.10) | collective-permute-done | bytes 524320 | tf_op jit(solution)/shard_map/ppermute | solution.py:259
  72.8 4.0 %collective-permute-start.4 = (f32[16,128,128]{2,1,0:T(8,128)}, f32[16,128,128]{2,1,0:T(8,128)S(1)}, u32[]{:S(2)}, u32[]{:S(2)}) collective-permute-start(f32[16,128,128]{2,1,0:T(8,128)} %get-tuple-element.23.rest_0_), channel_id=1, source_target_pairs={{0,48},{16,0},{32,16},{48,32},{64,112},{80,64},{96,80},{112,96},{1... | collective-permute-start | bytes 3145736 | tf_op jit(solution)/shard_map/ppermute | solution.py:250
  76.8 7.2 %collective-permute-done.13.refs_10_ = f32[2,512,128]{2,1,0:T(8,128)S(1)} collective-permute-done((f32[2,512,128]{2,1,0:T(8,128)}, f32[2,512,128]{2,1,0:T(8,128)S(1)}, u32[]{:S(2)}, u32[]{:S(2)}) %collective-permute-start.13) | collective-permute-done | bytes 524320 | tf_op jit(solution)/shard_map/ppermute | solution.py:259
  84.0 12.4 %collective-permute-start.11 = (f32[2,512,128]{2,1,0:T(8,128)}, f32[2,512,128]{2,1,0:T(8,128)S(1)}, u32[]{:S(2)}, u32[]{:S(2)}) collective-permute-start(f32[2,512,128]{2,1,0:T(8,128)} %get-tuple-element.26.refs_8_), channel_id=1, source_target_pairs={{0,12},{1,13},{2,14},{3,15},{4,0},{5,1},{6,2},{7,3},{8,4},{9,5},{1... | collective-permute-start | bytes 1572872 | tf_op jit(solution)/shard_map/ppermute | solution.py:259
  96.5 11.3 %collective-permute-done.11.refs_8_ = f32[2,512,128]{2,1,0:T(8,128)S(1)} collective-permute-done((f32[2,512,128]{2,1,0:T(8,128)}, f32[2,512,128]{2,1,0:T(8,128)S(1)}, u32[]{:S(2)}, u32[]{:S(2)}) %collective-permute-start.11) | collective-permute-done | bytes 524320 | tf_op jit(solution)/shard_map/ppermute | solution.py:259
  109.5 1.0 copy-done.13
  110.5 3.5 %regroup.2 = (f32[16,128,128]{2,1,0:T(8,128)}, f32[16,128,128]{2,1,0:T(8,128)}, f32[16,128,128]{2,1,0:T(8,128)}, f32[2,512,128]{2,1,0:T(8,128)}, f32[2,512,128]{...) custom-call(f32[16,128,128]{2,1,0:T(8,128)} %copy-done.13, ...), custom_call_target="tpu_custom_call", output_to_operand_aliasing={{3}: (7, {}), {4}: (8, {}), {5}: (9, {}), {6}: (10, {})} | custom-call | tf_op jit(solution)/shard_map/regroup/pallas_call | solution.py:153
  115.1 1.9 %collective-permute-start.14 = (f32[16,128,128]{2,1,0:T(8,128)}, f32[16,128,128]{2,1,0:T(8,128)S(1)}, u32[]{:S(2)}, u32[]{:S(2)}) collective-permute-start(f32[16,128,128]{2,1,0:T(8,128)} %get-tuple-element.27), channel_id=1, source_target_pairs={{0,16},{16,32},{32,48},{48,0},{64,80},{80,96},{96,112},{112,64},{1... | collective-permute-start | bytes 3145736 | tf_op jit(solution)/shard_map/ppermute | solution.py:250
  117.0 3.2 %collective-permute-start.15 = (f32[16,128,128]{2,1,0:T(8,128)}, f32[16,128,128]{2,1,0:T(8,128)S(1)}, u32[]{:S(2)}, u32[]{:S(2)}) collective-permute-start(f32[16,128,128]{2,1,0:T(8,128)} %get-tuple-element.28), channel_id=1, source_target_pairs={{0,48},{16,0},{32,16},{48,32},{64,112},{80,64},{96,80},{112,96},{1... | collective-permute-start | bytes 3145736 | tf_op jit(solution)/shard_map/ppermute | solution.py:250
  120.2 1.2 collective-permute-start.23
  121.5 0.8 copy-done.18
  123.0 7.4 %split_amplitudes.1.rest_4_.rest_3_ = bf16[2,2,4,2,512,256]{5,4,3,2,1,0:T(8,128)(2,1)} custom-call(f32[2,512,128]{2,1,0:T(8,128)} %refs_0_.1, f32[2,512,128]{2,1,0:T(8,128)} %get-tuple-element.24.refs_1_, f32[2,512,128]{2,1,0:T(8,128)} %get-tuple-element.29.refs_2_, f32[2,512,128]{2,1,0:T(8,128)} %get-tuple-element.25.refs_3_, f32[2,512,128]{2,1,0:T(8,128)} %copy-done.1, ...), custom_call_target="tpu_custom_call" | custom-call | flops 1048576 | bytes 25165824 | tf_op jit(solution)/shard_map/split_amplitudes/pallas_call | solution.py:177
  130.4 14.5 %product.3.refs_2_.rest_4_ = f32[512,2048]{1,0:T(8,128)} custom-call(s32[16,128]{1,0:T(8,128)} %get-tuple-element.21.meta_ref, f32[16,128,128]{2,1,0:T(8,128)} %get-tuple-element.23.rest_0_, f32[16,128,128]{2,1,0:T(8,128)} %copy-done.13, f32[16,128,128]{2,1,0:T(8,128)} %copy-done.12, f32[16,128,128]{2,1,0:T(8,128)} %copy-done.11, ...), custom_call_target="tpu_custom_call" | custom-call | flops 12884901888 | bytes 8388608 | tf_op jit(solution)/shard_map/product/pallas_call | solution.py:235
  144.9 1.0 copy-done.14
  145.9 1.0 copy-done.15
  146.8 2.2 %regroup.3 = (f32[5,128,128]{2,1,0:T(8,128)}, f32[5,128,128]{2,1,0:T(8,128)}, f32[6,128,128]{2,1,0:T(8,128)}) custom-call(f32[16,128,128]{2,1,0:T(8,128)} %copy-done.14, f32[16,128,128]{2,1,0:T(8,128)} %copy-done.15, f32[512,2048]{1,0:T(8,128)} %product.3.refs_2_.rest_4_), custom_call_target="tpu_custom_call" | custom-call | tf_op jit(solution)/shard_map/regroup/pallas_call | solution.py:153
  149.1 3.2 %collective-permute-start.21 = (f32[5,128,128]{2,1,0:T(8,128)}, f32[5,128,128]{2,1,0:T(8,128)S(1)}, u32[]{:S(2)}, u32[]{:S(2)}) collective-permute-start(f32[5,128,128]{2,1,0:T(8,128)} %get-tuple-element.34), channel_id=1, source_target_pairs={{0,48},{16,0},{32,16},{48,32},{64,112},{80,64},{96,80},{112,96},{1... | collective-permute-start | bytes 983048 | tf_op jit(solution)/shard_map/ppermute | solution.py:250
  152.4 0.8 collective-permute-start.22
  153.1 1.0 copy-done.23
  154.1 13.5 %product.4.rest_4_ = f32[512,2048]{1,0:T(8,128)} custom-call(s32[16,128]{1,0:T(8,128)} %get-tuple-element.21.meta_ref, f32[16,128,128]{2,1,0:T(8,128)} %copy-done.14, f32[16,128,128]{2,1,0:T(8,128)} %copy-done.15, f32[16,128,128]{2,1,0:T(8,128)} %copy-done.23, bf16[2,2,4,2,512,256]{5,4,3,2,1,0:T(8,128)(2,1)} %split_amplitudes.1.rest_4_.rest_3_, ...), custom_call_target="tpu_custom_call" | custom-call | flops 9663676416 | bytes 8388608 | tf_op jit(solution)/shard_map/product/pallas_call | solution.py:235
  169.2 8.9 %product.5 = f32[512,2048]{1,0:T(8,128)} custom-call(s32[16,128]{1,0:T(8,128)} %get-tuple-element.21.meta_ref, f32[5,128,128]{2,1,0:T(8,128)} %copy-done.21, f32[5,128,128]{2,1,0:T(8,128)} %copy-done.22, f32[6,128,128]{2,1,0:T(8,128)} %copy-done.20, bf16[2,2,4,2,512,256]{5,4,3,2,1,0:T(8,128)(2,1)} %split_amplitudes.1.rest_4_.rest_3_, f32[512,2048]{1,0:T(8,128)} %product.4.rest_4_), custom_call_target="tpu_custom_call" | custom-call | flops 3221225472 | bytes 8388608 | tf_op jit(solution)/shard_map/product/pallas_call | solution.py:235
  (75 shorter events, 6.8 us)
Async XLA Ops:
  6.6 46.6 %all-to-all-start = ((f32[16,2,128,128]{3,2,1,0:T(8,128)}), f32[16,2,128,128]{3,2,1,0:T(8,128)S(1)}, u32[]{:S(2)}, u32[]{:S(2)}) async-start(f32[16,2,128,128]{3,2,1,0:T(8,128)} %get-tuple-element.22), calls=%async_computation | async-start | bytes 4194304 | tf_op jit(solution)/shard_map/all_to_all | solution.py:272
  14.1 38.3 %collective-permute-start.2 = (f32[2,512,128]{2,1,0:T(8,128)}, f32[2,512,128]{2,1,0:T(8,128)S(1)}, u32[]{:S(2)}, u32[]{:S(2)}) collective-permute-start(f32[2,512,128]{2,1,0:T(8,128)} %refs_0_.1), channel_id=1, source_target_pairs={{0,4},{1,5},{2,6},{3,7},{4,8},{5,9},{6,10},{7,11},{8,12},{9,13},{1... | collective-permute-start | bytes 1572872 | tf_op jit(solution)/shard_map/ppermute | solution.py:259
  14.3 38.1 %collective-permute-start.1 = (f32[2,512,128]{2,1,0:T(8,128)}, f32[2,512,128]{2,1,0:T(8,128)S(1)}, u32[]{:S(2)}, u32[]{:S(2)}) collective-permute-start(f32[2,512,128]{2,1,0:T(8,128)} %refs_0_.1), channel_id=1, source_target_pairs={{0,12},{1,13},{2,14},{3,15},{4,0},{5,1},{6,2},{7,3},{8,4},{9,5},{1... | collective-permute-start | bytes 1572872 | tf_op jit(solution)/shard_map/ppermute | solution.py:259
  16.1 37.1 %collective-permute-start = (f32[2,512,128]{2,1,0:T(8,128)}, f32[2,512,128]{2,1,0:T(8,128)}, u32[]{:S(2)}, u32[]{:S(2)}) collective-permute-start(f32[2,512,128]{2,1,0:T(8,128)} %refs_0_.1), channel_id=1, source_target_pairs={{0,2},{1,3},{2,0},{3,1},{4,6},{5,7},{6,4},{7,5},{8,10},{9,11},{10,... | collective-permute-start | bytes 1572872 | tf_op jit(solution)/shard_map/ppermute | solution.py:263
  19.1 39.8 %collective-permute-start.6 = (f32[2,512,128]{2,1,0:T(8,128)}, f32[2,512,128]{2,1,0:T(8,128)S(1)}, u32[]{:S(2)}, u32[]{:S(2)}) collective-permute-start(f32[2,512,128]{2,1,0:T(8,128)} %refs_0_.1), channel_id=1, source_target_pairs={{0,1},{1,0},{2,3},{3,2},{4,5},{5,4},{6,7},{7,6},{8,9},{9,8},{10,11... | collective-permute-start | bytes 1572872 | tf_op jit(solution)/shard_map/ppermute | solution.py:263
  57.7 4.4 %collective-permute-start.7 = (f32[2,512,128]{2,1,0:T(8,128)}, f32[2,512,128]{2,1,0:T(8,128)S(1)}, u32[]{:S(2)}, u32[]{:S(2)}) collective-permute-start(f32[2,512,128]{2,1,0:T(8,128)} %get-tuple-element.24.refs_1_), channel_id=1, source_target_pairs={{0,1},{1,0},{2,3},{3,2},{4,5},{5,4},{6,7},{7,6},{8,9},{9,8},{10,11... | collective-permute-start | bytes 1572872 | tf_op jit(solution)/shard_map/ppermute | solution.py:263
  57.8 15.0 %collective-permute-start.10 = (f32[2,512,128]{2,1,0:T(8,128)}, f32[2,512,128]{2,1,0:T(8,128)S(1)}, u32[]{:S(2)}, u32[]{:S(2)}) collective-permute-start(f32[2,512,128]{2,1,0:T(8,128)} %get-tuple-element.25.refs_3_), channel_id=1, source_target_pairs={{0,4},{1,5},{2,6},{3,7},{4,8},{5,9},{6,10},{7,11},{8,12},{9,13},{1... | collective-permute-start | bytes 1572872 | tf_op jit(solution)/shard_map/ppermute | solution.py:259
  57.9 19.0 %collective-permute-start.8 = (f32[2,512,128]{2,1,0:T(8,128)}, f32[2,512,128]{2,1,0:T(8,128)S(1)}, u32[]{:S(2)}, u32[]{:S(2)}) collective-permute-start(f32[2,512,128]{2,1,0:T(8,128)} %get-tuple-element.25.refs_3_), channel_id=1, source_target_pairs={{0,1},{1,0},{2,3},{3,2},{4,5},{5,4},{6,7},{7,6},{8,9},{9,8},{10,11... | collective-permute-start | bytes 1572872 | tf_op jit(solution)/shard_map/ppermute | solution.py:263
  58.3 25.7 %collective-permute-start.13 = (f32[2,512,128]{2,1,0:T(8,128)}, f32[2,512,128]{2,1,0:T(8,128)S(1)}, u32[]{:S(2)}, u32[]{:S(2)}) collective-permute-start(f32[2,512,128]{2,1,0:T(8,128)} %get-tuple-element.26.refs_8_), channel_id=1, source_target_pairs={{0,4},{1,5},{2,6},{3,7},{4,8},{5,9},{6,10},{7,11},{8,12},{9,13},{1... | collective-permute-start | bytes 1572872 | tf_op jit(solution)/shard_map/ppermute | solution.py:259
  58.9 48.9 %copy-start.1 = (f32[2,512,128]{2,1,0:T(8,128)}, f32[2,512,128]{2,1,0:T(8,128)S(1)}, u32[]{:S(2)}) copy-start(f32[2,512,128]{2,1,0:T(8,128)S(1)} %collective-permute-done.6.refs_3_.refs_4_) | copy-start | bytes 1572868
  58.9 37.5 %collective-permute-start.12 = (f32[2,512,128]{2,1,0:T(8,128)}, f32[2,512,128]{2,1,0:T(8,128)S(1)}, u32[]{:S(2)}, u32[]{:S(2)}) collective-permute-start(f32[2,512,128]{2,1,0:T(8,128)} %get-tuple-element.26.refs_8_), channel_id=1, source_target_pairs={{0,8},{1,9},{2,10},{3,11},{4,12},{5,13},{6,14},{7,15},{8,0},{9,1},... | collective-permute-start | bytes 1572872 | tf_op jit(solution)/shard_map/ppermute | solution.py:259
  62.1 45.7 %copy-start.2 = (f32[2,512,128]{2,1,0:T(8,128)}, f32[2,512,128]{2,1,0:T(8,128)S(1)}, u32[]{:S(2)}) copy-start(f32[2,512,128]{2,1,0:T(8,128)S(1)} %collective-permute-done.7.refs_4_.refs_5_) | copy-start | bytes 1572868
  62.1 45.6 %collective-permute-start.5 = (f32[16,128,128]{2,1,0:T(8,128)}, f32[16,128,128]{2,1,0:T(8,128)S(1)}, u32[]{:S(2)}, u32[]{:S(2)}) collective-permute-start(f32[16,128,128]{2,1,0:T(8,128)} %get-tuple-element.23.rest_0_), channel_id=1, source_target_pairs={{0,64},{16,80},{32,96},{48,112},{64,0},{80,16},{96,32},{112,48},{1... | collective-permute-start | bytes 3145736 | tf_op jit(solution)/shard_map/ppermute | solution.py:254
  72.8 35.0 %copy-start.5 = (f32[2,512,128]{2,1,0:T(8,128)}, f32[2,512,128]{2,1,0:T(8,128)S(1)}, u32[]{:S(2)}) copy-start(f32[2,512,128]{2,1,0:T(8,128)S(1)} %collective-permute-done.10.refs_7_) | copy-start | bytes 1572868
  72.8 35.0 %collective-permute-start.4 = (f32[16,128,128]{2,1,0:T(8,128)}, f32[16,128,128]{2,1,0:T(8,128)S(1)}, u32[]{:S(2)}, u32[]{:S(2)}) collective-permute-start(f32[16,128,128]{2,1,0:T(8,128)} %get-tuple-element.23.rest_0_), channel_id=1, source_target_pairs={{0,48},{16,0},{32,16},{48,32},{64,112},{80,64},{96,80},{112,96},{1... | collective-permute-start | bytes 3145736 | tf_op jit(solution)/shard_map/ppermute | solution.py:250
  76.8 31.0 %copy-start.3 = (f32[2,512,128]{2,1,0:T(8,128)}, f32[2,512,128]{2,1,0:T(8,128)S(1)}, u32[]{:S(2)}) copy-start(f32[2,512,128]{2,1,0:T(8,128)S(1)} %collective-permute-done.8.refs_5_.refs_7_) | copy-start | bytes 1572868
  76.8 31.0 %collective-permute-start.3 = (f32[16,128,128]{2,1,0:T(8,128)}, f32[16,128,128]{2,1,0:T(8,128)S(1)}, u32[]{:S(2)}, u32[]{:S(2)}) collective-permute-start(f32[16,128,128]{2,1,0:T(8,128)} %get-tuple-element.23.rest_0_), channel_id=1, source_target_pairs={{0,16},{16,32},{32,48},{48,0},{64,80},{80,96},{96,112},{112,64},{1... | collective-permute-start | bytes 3145736 | tf_op jit(solution)/shard_map/ppermute | solution.py:250
  84.0 23.8 %copy-start.6 = (f32[2,512,128]{2,1,0:T(8,128)}, f32[2,512,128]{2,1,0:T(8,128)S(1)}, u32[]{:S(2)}) copy-start(f32[2,512,128]{2,1,0:T(8,128)S(1)} %collective-permute-done.13.refs_10_) | copy-start | bytes 1572868
  84.0 23.7 %collective-permute-start.11 = (f32[2,512,128]{2,1,0:T(8,128)}, f32[2,512,128]{2,1,0:T(8,128)S(1)}, u32[]{:S(2)}, u32[]{:S(2)}) collective-permute-start(f32[2,512,128]{2,1,0:T(8,128)} %get-tuple-element.26.refs_8_), channel_id=1, source_target_pairs={{0,12},{1,13},{2,14},{3,15},{4,0},{5,1},{6,2},{7,3},{8,4},{9,5},{1... | collective-permute-start | bytes 1572872 | tf_op jit(solution)/shard_map/ppermute | solution.py:259
  96.5 11.4 %copy-start.7 = (f32[2,512,128]{2,1,0:T(8,128)}, f32[2,512,128]{2,1,0:T(8,128)S(1)}, u32[]{:S(2)}) copy-start(f32[2,512,128]{2,1,0:T(8,128)S(1)} %collective-permute-done.12.refs_9_) | copy-start | bytes 1572868
  96.5 11.3 %collective-permute-start.9 = (f32[2,512,128]{2,1,0:T(8,128)}, f32[2,512,128]{2,1,0:T(8,128)S(1)}, u32[]{:S(2)}, u32[]{:S(2)}) collective-permute-start(f32[2,512,128]{2,1,0:T(8,128)} %get-tuple-element.26.refs_8_), channel_id=1, source_target_pairs={{0,1},{1,0},{2,3},{3,2},{4,5},{5,4},{6,7},{7,6},{8,9},{9,8},{10,11... | collective-permute-start | bytes 1572872 | tf_op jit(solution)/shard_map/ppermute | solution.py:263
  114.0 3.0 %collective-permute-start.16 = (f32[2,512,128]{2,1,0:T(8,128)}, f32[2,512,128]{2,1,0:T(8,128)S(1)}, u32[]{:S(2)}, u32[]{:S(2)}) collective-permute-start(f32[2,512,128]{2,1,0:T(8,128)} %get-tuple-element.29.refs_2_), channel_id=1, source_target_pairs={{0,1},{1,0},{2,3},{3,2},{4,5},{5,4},{6,7},{7,6},{8,9},{9,8},{10,11... | collective-permute-start | bytes 1572872 | tf_op jit(solution)/shard_map/ppermute | solution.py:263
  114.1 6.1 %collective-permute-start.17 = (f32[2,512,128]{2,1,0:T(8,128)}, f32[2,512,128]{2,1,0:T(8,128)S(1)}, u32[]{:S(2)}, u32[]{:S(2)}) collective-permute-start(f32[2,512,128]{2,1,0:T(8,128)} %get-tuple-element.30.refs_9_), channel_id=1, source_target_pairs={{0,1},{1,0},{2,3},{3,2},{4,5},{5,4},{6,7},{7,6},{8,9},{9,8},{10,11... | collective-permute-start | bytes 1572872 | tf_op jit(solution)/shard_map/ppermute | solution.py:263
  114.6 6.9 %collective-permute-start.18 = (f32[2,512,128]{2,1,0:T(8,128)}, f32[2,512,128]{2,1,0:T(8,128)S(1)}, u32[]{:S(2)}, u32[]{:S(2)}) collective-permute-start(f32[2,512,128]{2,1,0:T(8,128)} %get-tuple-element.31.refs_10_), channel_id=1, source_target_pairs={{0,1},{1,0},{2,3},{3,2},{4,5},{5,4},{6,7},{7,6},{8,9},{9,8},{10,11... | collective-permute-start | bytes 1572872 | tf_op jit(solution)/shard_map/ppermute | solution.py:263
  114.7 6.8 %collective-permute-start.19 = (f32[2,512,128]{2,1,0:T(8,128)}, f32[2,512,128]{2,1,0:T(8,128)S(1)}, u32[]{:S(2)}, u32[]{:S(2)}) collective-permute-start(f32[2,512,128]{2,1,0:T(8,128)} %get-tuple-element.32.refs_11_), channel_id=1, source_target_pairs={{0,1},{1,0},{2,3},{3,2},{4,5},{5,4},{6,7},{7,6},{8,9},{9,8},{10,11... | collective-permute-start | bytes 1572872 | tf_op jit(solution)/shard_map/ppermute | solution.py:263
  115.1 29.8 %collective-permute-start.14 = (f32[16,128,128]{2,1,0:T(8,128)}, f32[16,128,128]{2,1,0:T(8,128)S(1)}, u32[]{:S(2)}, u32[]{:S(2)}) collective-permute-start(f32[16,128,128]{2,1,0:T(8,128)} %get-tuple-element.27), channel_id=1, source_target_pairs={{0,16},{16,32},{32,48},{48,0},{64,80},{80,96},{96,112},{112,64},{1... | collective-permute-start | bytes 3145736 | tf_op jit(solution)/shard_map/ppermute | solution.py:250
  117.0 4.4 %copy-start.16 = (f32[2,512,128]{2,1,0:T(8,128)}, f32[2,512,128]{2,1,0:T(8,128)S(1)}, u32[]{:S(2)}) copy-start(f32[2,512,128]{2,1,0:T(8,128)S(1)} %collective-permute-done.16.refs_6_) | copy-start | bytes 1572868
  117.0 27.9 %collective-permute-start.15 = (f32[16,128,128]{2,1,0:T(8,128)}, f32[16,128,128]{2,1,0:T(8,128)S(1)}, u32[]{:S(2)}, u32[]{:S(2)}) collective-permute-start(f32[16,128,128]{2,1,0:T(8,128)} %get-tuple-element.28), channel_id=1, source_target_pairs={{0,48},{16,0},{32,16},{48,32},{64,112},{80,64},{96,80},{112,96},{1... | collective-permute-start | bytes 3145736 | tf_op jit(solution)/shard_map/ppermute | solution.py:250
  120.2 32.9 %collective-permute-start.23 = (f32[16,128,128]{2,1,0:T(8,128)}, f32[16,128,128]{2,1,0:T(8,128)S(1)}, u32[]{:S(2)}, u32[]{:S(2)}) collective-permute-start(f32[16,128,128]{2,1,0:T(8,128)} %get-tuple-element.36), channel_id=1, source_target_pairs={{0,64},{16,80},{32,96},{48,112},{64,0},{80,16},{96,32},{112,48},{1... | collective-permute-start | bytes 3145736 | tf_op jit(solution)/shard_map/ppermute | solution.py:254
  149.0 18.6 %collective-permute-start.20 = (f32[5,128,128]{2,1,0:T(8,128)}, f32[5,128,128]{2,1,0:T(8,128)S(1)}, u32[]{:S(2)}, u32[]{:S(2)}) collective-permute-start(f32[5,128,128]{2,1,0:T(8,128)} %get-tuple-element.33), channel_id=1, source_target_pairs={{0,16},{16,32},{32,48},{48,0},{64,80},{80,96},{96,112},{112,64},{1... | collective-permute-start | bytes 983048 | tf_op jit(solution)/shard_map/ppermute | solution.py:250
  149.1 18.5 %collective-permute-start.21 = (f32[5,128,128]{2,1,0:T(8,128)}, f32[5,128,128]{2,1,0:T(8,128)S(1)}, u32[]{:S(2)}, u32[]{:S(2)}) collective-permute-start(f32[5,128,128]{2,1,0:T(8,128)} %get-tuple-element.34), channel_id=1, source_target_pairs={{0,48},{16,0},{32,16},{48,32},{64,112},{80,64},{96,80},{112,96},{1... | collective-permute-start | bytes 983048 | tf_op jit(solution)/shard_map/ppermute | solution.py:250
  152.4 15.3 %collective-permute-start.22 = (f32[6,128,128]{2,1,0:T(8,128)}, f32[6,128,128]{2,1,0:T(8,128)S(1)}, u32[]{:S(2)}, u32[]{:S(2)}) collective-permute-start(f32[6,128,128]{2,1,0:T(8,128)} %get-tuple-element.35), channel_id=1, source_target_pairs={{0,64},{16,80},{32,96},{48,112},{64,0},{80,16},{96,32},{112,48},{1... | collective-permute-start | bytes 1179656 | tf_op jit(solution)/shard_map/ppermute | solution.py:254
  (17 other events, 17.0 us)

commit v2 on v1

--- a/solution.py
+++ b/solution.py
@@ -16,7 +16,8 @@
 HOLD = 64
 CHUNK = HOLD // N_ROW
 LANES = 128
-VMEM_LIMIT = 56 * 1024 * 1024
+VMEM_LIMIT = 26 * 1024 * 1024
+SMALL_LIMIT = 12 * 1024 * 1024
 
 
 def route_kernel(reader_ref, row_ref, column_ref, tiles_ref, meta_ref, *rest):
@@ -96,41 +97,43 @@
     )(readers, rows, columns, tiles)
 
 
-def compact_kernel(passed, meta_ref, arrived_ref, *rest):
-    out_ref, sems = rest[-2 - passed], rest[-1]
+def compact_kernel(meta_ref, arrived_ref, amp_ref, side_ref, left_ref, far_ref, out_ref, minus_ref, plus_ref, sems):
     me_row = lax.axis_index("row")
     copies = []
+
+    def copy(source, target):
+        copies.append(pltpu.make_async_copy(source, target, sems.at[len(copies)]))
+        copies[-1].start()
+
     for s in range(STEPS):
         for j in range(CHUNK):
             holder = meta_ref[s * 8 + 1, j * N_ROW + me_row]
-            at = len(copies)
-            copies.append(pltpu.make_async_copy(arrived_ref.at[holder, s], out_ref.at[at], sems.at[at]))
-            copies[-1].start()
-    for copy in copies:
-        copy.wait()
-
-
-def compact(meta, arrived, passed):
+            copy(arrived_ref.at[holder, s], out_ref.at[s * CHUNK + j])
+    for n, ref in enumerate((amp_ref, side_ref)):
+        copy(ref, minus_ref.at[pl.ds(n * STEPS, STEPS)])
+    for n, ref in enumerate((left_ref, side_ref)):
+        copy(ref, plus_ref.at[pl.ds(n * STEPS, STEPS)])
+    for one in copies:
+        one.wait()
+
+
+def compact(meta, arrived, amplitudes, side, amp_left, side_far):
     tiles = STEPS * CHUNK
-    hbm = pl.BlockSpec(memory_space=pltpu.HBM)
-    return pl.pallas_call(
-        functools.partial(compact_kernel, len(passed)),
-        out_shape=[jax.ShapeDtypeStruct((tiles, TILE, TILE), jnp.float32)]
-        + [jax.ShapeDtypeStruct(p.shape, p.dtype) for p in passed],
-        grid_spec=pltpu.PrefetchScalarGridSpec(
-            num_scalar_prefetch=1,
-            grid=(1,),
-            in_specs=[hbm] * (1 + len(passed)),
-            out_specs=[pl.BlockSpec((tiles, TILE, TILE), lambda n, meta: (0, 0, 0))] + [hbm] * len(passed),
-            scratch_shapes=[pltpu.SemaphoreType.DMA((tiles,))],
-        ),
-        input_output_aliases={2 + n: 1 + n for n in range(len(passed))},
+    hbm, vmem = pl.BlockSpec(memory_space=pltpu.HBM), pl.BlockSpec(memory_space=pltpu.VMEM)
+    pair = jax.ShapeDtypeStruct((2 * STEPS,) + amplitudes.shape[1:], jnp.float32)
+    return pl.pallas_call(
+        compact_kernel,
+        out_shape=[jax.ShapeDtypeStruct((tiles, TILE, TILE), jnp.float32), pair, pair],
+        in_specs=[pl.BlockSpec(memory_space=pltpu.SMEM)] + [hbm] * 5,
+        out_specs=[vmem] * 3,
+        scratch_shapes=[pltpu.SemaphoreType.DMA((tiles + 4,))],
+        compiler_params=pltpu.CompilerParams(vmem_limit_bytes=SMALL_LIMIT),
         name="compact",
-    )(meta, arrived, *passed)
-
-
-def regroup_kernel(plan, passed, *refs):
-    outs, sems = refs[-1 - passed - len(plan) : -1 - passed], refs[-1]
+    )(meta, arrived, amplitudes, side, amp_left, side_far)
+
+
+def regroup_kernel(plan, *refs):
+    outs, sems = refs[-1 - len(plan) : -1], refs[-1]
     copies = []
     for out, parts in zip(outs, plan):
         begin = 0
@@ -146,44 +149,44 @@
         copy.wait()
 
 
-def regroup(chunks, plan, passed=(), earlier=()):
-    any_space, hbm = pl.BlockSpec(memory_space=pl.ANY), pl.BlockSpec(memory_space=pltpu.HBM)
-    shapes = [(sum(size for _, _, size in parts),) + chunks[0].shape[1:] for parts in plan]
-    before = len(chunks) + len(earlier)
-    return pl.pallas_call(
-        functools.partial(regroup_kernel, plan, len(passed)),
-        out_shape=[jax.ShapeDtypeStruct(shape, jnp.float32) for shape in shapes]
-        + [jax.ShapeDtypeStruct(p.shape, p.dtype) for p in passed],
-        in_specs=[any_space] * before + [hbm] * len(passed),
-        out_specs=[pl.BlockSpec(memory_space=pltpu.VMEM)] * len(plan) + [hbm] * len(passed),
+def regroup(chunks, plan, *earlier):
+    any_space = pl.BlockSpec(memory_space=pl.ANY)
+    shapes = [
+        (sum(size for _, _, size in parts),) + chunks[parts[0][0]].shape[1:] for parts in plan
+    ]
+    return pl.pallas_call(
+        functools.partial(regroup_kernel, plan),
+        out_shape=[jax.ShapeDtypeStruct(shape, jnp.float32) for shape in shapes],
+        in_specs=[any_space] * (len(chunks) + len(earlier)),
+        out_specs=[pl.BlockSpec(memory_space=pltpu.VMEM)] * len(plan),
         scratch_shapes=[pltpu.SemaphoreType.DMA((sum(len(parts) for parts in plan),))],
-        input_output_aliases={before + n: len(plan) + n for n in range(len(passed))},
-        compiler_params=pltpu.CompilerParams(vmem_limit_bytes=VMEM_LIMIT),
+        compiler_params=pltpu.CompilerParams(vmem_limit_bytes=SMALL_LIMIT),
         name="regroup",
-    )(*chunks, *earlier, *passed)
-
-
-def split_kernel(*refs):
-    out_ref = refs[-1]
-    for at, ref in enumerate(refs[:-1]):
-        value = ref[0]
-        high = value.astype(jnp.bfloat16)
-        out_ref[at // 8, at // 4 % 2, at % 4, 0, :, :TILE] = high
-        out_ref[at // 8, at // 4 % 2, at % 4, 0, :, TILE:] = (value - high.astype(jnp.float32)).astype(jnp.bfloat16)
-
-
-def split_amplitudes(pieces):
-    panels, rows = pieces[0].shape[:2]
+    )(*chunks, *earlier)
+
+
+def split_kernel(amp_ref, other_ref, out_ref):
+    for core, ref in enumerate((amp_ref, other_ref)):
+        for n in range(ref.shape[0]):
+            value = ref[n]
+            high = value.astype(jnp.bfloat16)
+            out_ref[core, n, :, :TILE] = high
+            out_ref[core, n, :, TILE:] = (value - high.astype(jnp.float32)).astype(jnp.bfloat16)
+
+
+def split_amplitudes(ours, others):
+    count, rows = ours.shape[:2]
+    block = pl.BlockSpec((2, rows, TILE), lambda n: (n, 0, 0))
     return pl.pallas_call(
         split_kernel,
-        out_shape=jax.ShapeDtypeStruct((2, 2, 4, panels, rows, 2 * TILE), jnp.bfloat16),
-        grid=(panels, 2),
-        in_specs=[pl.BlockSpec((1, rows // 2, TILE), lambda s, n: (s, n, 0))] * 16,
-        out_specs=pl.BlockSpec((2, 2, 4, 1, rows // 2, 2 * TILE), lambda s, n: (0, 0, 0, s, n, 0)),
-        compiler_params=pltpu.CompilerParams(vmem_limit_bytes=VMEM_LIMIT),
+        out_shape=jax.ShapeDtypeStruct((2, count, rows, 2 * TILE), jnp.bfloat16),
+        grid=(count // 2,),
+        in_specs=[block, block],
+        out_specs=pl.BlockSpec((2, 2, rows, 2 * TILE), lambda n: (0, n, 0, 0)),
+        compiler_params=pltpu.CompilerParams(vmem_limit_bytes=SMALL_LIMIT),
         cost_estimate=pl.CostEstimate(flops=2**20, bytes_accessed=24 * 2**20, transcendentals=0),
         name="split_amplitudes",
-    )(*pieces)
+    )(ours, others)
 
 
 def product_kernel(places, has_start, meta_ref, *rest):
@@ -207,7 +210,7 @@
                 s = number // CHUNK
                 code = meta_ref[s * 8, (number % CHUNK) * N_ROW + source]
                 column = code // NT_DEV
-                away = (column // 4 + 4 - me_col // 4) % 4
+                away = ((column // 4 + 4 - me_col // 4) % 4) * 2 + ((column ^ me_col) // 2) % 2
                 tile = ref[at + m]
                 high = tile.astype(jnp.bfloat16)
                 low = (tile - high.astype(jnp.float32)).astype(jnp.bfloat16)
@@ -217,7 +220,7 @@
                 for begin in range(0, out_ref.shape[0], block):
                     rows = pl.ds(begin, block)
                     both = jnp.dot(
-                        amp_ref[((column ^ me_col) // 2) % 2, (column ^ me_col) % 2, away, s, rows],
+                        amp_ref[(column ^ me_col) % 2, away * STEPS + s, rows],
                         wide,
                         preferred_element_type=jnp.float32,
                     )
@@ -229,7 +232,7 @@
 
 def product(meta, chunks, places, amps, start=None):
     vmem = pl.BlockSpec(memory_space=pltpu.VMEM)
-    rows = amps.shape[4]
+    rows = amps.shape[2]
     operands = list(chunks) + [amps] + ([] if start is None else [start])
     tiles = sum(c.shape[0] for c in chunks)
     return pl.pallas_call(
@@ -268,29 +271,30 @@
     meta, sent = route(
         tile_reader.reshape(held), tile_rows.reshape(held), tile_column.reshape(held), integrals
     )
-    side, amp_right, amp_left = flip(amplitudes, 2), along_x(amplitudes, -1), along_x(amplitudes, 1)
+    side, amp_left = flip(amplitudes, 2), along_x(amplitudes, 1)
+    side_far = lax.ppermute(amplitudes, "col", [(c, (c ^ 2) ^ 8) for c in range(N_COL)])
     arrived = lax.all_to_all(sent, "col", split_axis=0, concat_axis=0, tiled=True)
-    own, side, amp_right, amp_left = compact(meta, arrived, (side, amp_right, amp_left))
+    own, minus, plus = compact(meta, arrived, amplitudes, side, amp_left, side_far)
 
     left, right, other = along_z(own, 1), along_z(own, -1), across_y(own)
-    side_around = [along_x(side, step) for step in (-1, 2, 1)]
-    amp_far = along_x(amp_left, 1)
-    flipped = [flip(p, 1) for p in (amplitudes, amp_right, amp_left, side)]
-
-    up, down, across, amp_far, *side_around = regroup(
-        [left, right, other],
-        [[(0, 0, 8), (2, 0, 8)], [(1, 8, 8), (2, 8, 8)], [(0, 8, 8), (1, 0, 8)]],
-        [amp_far] + side_around,
-        flipped,
+    from_right, from_left = along_x(minus, -1), along_x(plus, 1)
+
+    up, down, across, ours = regroup(
+        [left, right, other, minus, from_right, from_left, side_far, plus],
+        [
+            [(0, 0, 8), (2, 0, 8)],
+            [(1, 8, 8), (2, 8, 8)],
+            [(0, 8, 8), (1, 0, 8)],
+            [(3, 0, 4), (4, 0, 4), (5, 0, 2), (6, 0, 2), (7, 0, 2), (5, 2, 2)],
+        ],
     )
     up, down, across = along_z(up, 1), along_z(down, -1), across_y(across)
-    flipped = flipped[:2] + [flip(amp_far, 1)] + flipped[2:] + [flip(p, 1) for p in side_around]
-    amps = split_amplitudes([amplitudes, amp_right, amp_far, amp_left] + flipped[:4] + [side] + side_around + flipped[4:])
+    amps = split_amplitudes(ours, flip(ours, 1))
     places = [[(dy, dz, 0, 16)] for dy, dz in ((0, 0), (0, 3), (0, 1), (1, 0))]
     ladder = product(meta, [own, left, right, other], places, amps)
 
     far_up, far_down, far_across = regroup(
-        [up, down], [[(0, 8, 5)], [(1, 11, 5)], [(0, 5, 3), (1, 0, 3)]], (), [ladder]
+        [up, down], [[(0, 8, 5)], [(1, 11, 5)], [(0, 5, 3), (1, 0, 3)]], ladder
     )
     far_up, far_down, far_across = along_z(far_up, 1), along_z(far_down, -1), across_y(far_across)
     places = [

time: 181 us -> 150 us (0.83)
  Pallas kernels: 58.4 us -> 31.1 us
  waiting for transfers between devices: 61.2 us -> 82.1 us
  starting transfers between devices: 46.1 us -> 30.5 us
  local copies, waits for them, and re-layouts: 12.2 us -> 5.01 us
    pallas_call x3, Pallas kernels: 36.8 us -> 19.7 us  [product(): pl.pallas_call(functools.partial(product_kernel, places, start is not Non...]
    ppermute x6 -> x3, starting transfers between devices: 18.3 us -> 3.47 us  [along_x(): return lax.ppermute(value, 'col', pairs)]
    ppermute x6, waiting for transfers between devices: 0.02 us -> 14.7 us  [along_z(): return lax.ppermute(value, 'row', pairs)]
    ppermute x9 -> x2, waiting for transfers between devices: 0.02 us -> 12.5 us  [flip(): return lax.ppermute(value, 'col', [(c, c ^ bit) for c in range(N_COL)])]
    ppermute x6 -> x3, waiting for transfers between devices: 61.2 us -> 50.7 us  [along_x(): return lax.ppermute(value, 'col', pairs)]
    pallas_call x4, Pallas kernels: 16.3 us -> 6.15 us  [the longest x1 2.48 us: compact(): pl.pallas_call(compact_kernel, out_shape=[jax.ShapeDtypeStruct((tiles, TI...]
    unnamed x48 -> x12, local copies, waits for them, and re-layouts: 10.8 us -> 3.71 us
    ppermute x3, waiting for transfers between devices: 0.01 us -> 4.14 us  [across_y(): return lax.ppermute(value, 'row', [(i, i ^ Z) for i in range(N_ROW)])]
  transfers between devices with their start and end apart: 25 -> 16, of which waited for: 4 -> 9; matrix products, arithmetic and copies ran while one was open for 0% -> 0% of each run, Pallas kernels for 23% -> 12%
where the time goes in v2:
time: 150 us; the launch traced here: 149 us
  waiting for transfers between devices  82.1 us (55%)
  Pallas kernels  31.1 us (21%)
  starting transfers between devices  30.5 us (20%)
  local copies, waits for them, and re-layouts  5.01 us (3%)
    ppermute x3, waiting for transfers between devices, along_x(): return lax.ppermute(value, 'col', pairs)  50.7 us
    pallas_call x3, Pallas kernels, product(): pl.pallas_call(functools.partial(product_kernel, places, start is not Non...  19.7 us
    ppermute x6, waiting for transfers between devices, along_z(): return lax.ppermute(value, 'row', pairs)  14.7 us
    ppermute x2, waiting for transfers between devices, flip(): return lax.ppermute(value, 'col', [(c, c ^ bit) for c in range(N_COL)])  12.5 us
    ppermute x6, starting transfers between devices, along_z(): return lax.ppermute(value, 'row', pairs)  10.6 us
    all_to_all x1, starting transfers between devices, shards(): lax.all_to_all(sent, 'col', split_axis=0, concat_axis=0, tiled=True)  7.64 us
    pallas_call x1, Pallas kernels, route(): pl.pallas_call(route_kernel, out_shape=(jax.ShapeDtypeStruct((8 * STEPS,...  5.3 us
    ppermute x3, waiting for transfers between devices, across_y(): return lax.ppermute(value, 'row', [(i, i ^ Z) for i in range(N_ROW)])  4.14 us
  transfers between devices with their start and end apart: 16, of which 9 were waited for; matrix products, arithmetic and copies ran while one was open for 0% of the time, Pallas kernels for 12%

profile of v2, /device:TPU:6, one launch (start us, length us, event | category | flops | bytes accessed | tf_op | source)
XLA Modules:
  0.0 148.8 jit_solution(16477902407650111441)
XLA Ops:
  0.0 1.3 copy_bitcast_fusion
  1.3 5.3 %route.1 = (s32[16,128]{1,0:T(8,128)}, f32[16,2,128,128]{3,2,1,0:T(8,128)}) custom-call(s32[2,8,128]{2,1,0:T(8,128)} %bitcast.7, s32[2,8,128]{2,1,0:T(8,128)} %get-tuple-element.30.row_ref, s32[2,8,128]{2,1,0:T(8,128)} %get-tuple-element.29.column_ref, f32[2,64,128,128]{3,2,1,0:T(8,128)} %tiles_ref.1), custom_call_target="tpu_custom_call" | custom-call | tf_op jit(solution)/shard_map/route/pallas_call | solution.py:83
  6.6 7.6 %all-to-all-start = ((f32[16,2,128,128]{3,2,1,0:T(8,128)}), f32[16,2,128,128]{3,2,1,0:T(8,128)S(1)}, u32[]{:S(2)}, u32[]{:S(2)}) async-start(f32[16,2,128,128]{3,2,1,0:T(8,128)} %get-tuple-element.18), calls=%async_computation | async-start | bytes 4194304 | tf_op jit(solution)/shard_map/all_to_all | solution.py:276
  14.5 3.4 %collective-permute-start = (f32[2,512,128]{2,1,0:T(8,128)S(1)}, f32[2,512,128]{2,1,0:T(8,128)S(1)}, u32[]{:S(2)}, u32[]{:S(2)}) collective-permute-start(f32[2,512,128]{2,1,0:T(8,128)S(1)} %copy-done), channel_id=1, source_target_pairs={{0,2},{1,3},{2,0},{3,1},{4,6},{5,7},{6,4},{7,5},{8,10},{9,11},{10,... | collective-permute-start | bytes 1572872 | tf_op jit(solution)/shard_map/ppermute | solution.py:266
  17.9 2.4 %collective-permute-start.2 = (f32[2,512,128]{2,1,0:T(8,128)S(1)}, f32[2,512,128]{2,1,0:T(8,128)S(1)}, u32[]{:S(2)}, u32[]{:S(2)}) collective-permute-start(f32[2,512,128]{2,1,0:T(8,128)S(1)} %copy-done), channel_id=1, source_target_pairs={{0,10},{1,11},{2,8},{3,9},{4,14},{5,15},{6,12},{7,13},{8,2},{9,3},... | collective-permute-start | bytes 1572872 | tf_op jit(solution)/shard_map/ppermute | solution.py:275
  20.2 32.8 %collective-permute-done.1.left_ref = f32[2,512,128]{2,1,0:T(8,128)S(1)} collective-permute-done((f32[2,512,128]{2,1,0:T(8,128)S(1)}, f32[2,512,128]{2,1,0:T(8,128)S(1)}, u32[]{:S(2)}, u32[]{:S(2)}) %collective-permute-start.1) | collective-permute-done | bytes 524320 | tf_op jit(solution)/shard_map/ppermute | solution.py:262
  53.0 0.8 copy-done.1
  53.8 9.6 %collective-permute-done.side_ref = f32[2,512,128]{2,1,0:T(8,128)S(1)} collective-permute-done((f32[2,512,128]{2,1,0:T(8,128)S(1)}, f32[2,512,128]{2,1,0:T(8,128)S(1)}, u32[]{:S(2)}, u32[]{:S(2)}) %collective-permute-start) | collective-permute-done | bytes 524320 | tf_op jit(solution)/shard_map/ppermute | solution.py:266
  63.4 0.8 copy-done.3
  64.2 1.0 copy-done.2
  65.3 1.0 copy-done.4
  66.3 2.5 %compact.1 = (f32[16,128,128]{2,1,0:T(8,128)S(1)}, f32[4,512,128]{2,1,0:T(8,128)S(1)}, f32[4,512,128]{2,1,0:T(8,128)S(1)}) custom-call(s32[16,128]{1,0:T(8,128)S(1)} %copy-done.5, f32[16,2,128,128]{3,2,1,0:T(8,128)S(1)} %all-to-all-done.arrived_ref, f32[2,512,128]{2,1,0:T(8,128)S(1)} %copy-done, f32[2,512,128]{2,1,0:T(8,128)S(1)} %copy-done.4, ...), custom_call_target="tpu_custom_call" | custom-call | tf_op jit(solution)/shard_map/compact/pallas_call | solution.py:124
  68.8 1.1 collective-permute-start.6
  69.9 2.2 %collective-permute-start.7 = (f32[4,512,128]{2,1,0:T(8,128)S(1)}, f32[4,512,128]{2,1,0:T(8,128)S(1)}, u32[]{:S(2)}, u32[]{:S(2)}) collective-permute-start(f32[4,512,128]{2,1,0:T(8,128)S(1)} %get-tuple-element.21.refs_7_), channel_id=1, source_target_pairs={{0,4},{1,5},{2,6},{3,7},{4,8},{5,9},{6,10},{7,11},{8,12},{9,13},{1... | collective-permute-start | bytes 3145736 | tf_op jit(solution)/shard_map/ppermute | solution.py:262
  72.1 1.2 collective-permute-start.5
  73.3 4.0 %collective-permute-start.4 = (f32[16,128,128]{2,1,0:T(8,128)S(1)}, f32[16,128,128]{2,1,0:T(8,128)S(1)}, u32[]{:S(2)}, u32[]{:S(2)}) collective-permute-start(f32[16,128,128]{2,1,0:T(8,128)S(1)} %get-tuple-element.19.rest_0_), channel_id=1, source_target_pairs={{0,48},{16,0},{32,16},{48,32},{64,112},{80,64},{96,80},{112,96},{1... | collective-permute-start | bytes 3145736 | tf_op jit(solution)/shard_map/ppermute | solution.py:253
  77.3 17.9 %collective-permute-done.6.refs_4_ = f32[4,512,128]{2,1,0:T(8,128)S(1)} collective-permute-done((f32[4,512,128]{2,1,0:T(8,128)S(1)}, f32[4,512,128]{2,1,0:T(8,128)S(1)}, u32[]{:S(2)}, u32[]{:S(2)}) %collective-permute-start.6) | collective-permute-done | bytes 1048608 | tf_op jit(solution)/shard_map/ppermute | solution.py:262
  95.2 1.5 collective-permute-done.5.refs_2_.rest_3_
  96.7 2.4 %collective-permute-done.4.refs_1_.rest_2_ = f32[16,128,128]{2,1,0:T(8,128)S(1)} collective-permute-done((f32[16,128,128]{2,1,0:T(8,128)S(1)}, f32[16,128,128]{2,1,0:T(8,128)S(1)}, u32[]{:S(2)}, u32[]{:S(2)}) %collective-permute-start.4) | collective-permute-done | bytes 1048608 | tf_op jit(solution)/shard_map/ppermute | solution.py:253
  99.1 3.4 %collective-permute-done.3.refs_0_.rest_1_ = f32[16,128,128]{2,1,0:T(8,128)S(1)} collective-permute-done((f32[16,128,128]{2,1,0:T(8,128)S(1)}, f32[16,128,128]{2,1,0:T(8,128)S(1)}, u32[]{:S(2)}, u32[]{:S(2)}) %collective-permute-start.3) | collective-permute-done | bytes 1048608 | tf_op jit(solution)/shard_map/ppermute | solution.py:253
  103.3 3.2 %collective-permute-start.9 = (f32[16,128,128]{2,1,0:T(8,128)S(1)}, f32[16,128,128]{2,1,0:T(8,128)S(1)}, u32[]{:S(2)}, u32[]{:S(2)}) collective-permute-start(f32[16,128,128]{2,1,0:T(8,128)S(1)} %get-tuple-element.23), channel_id=1, source_target_pairs={{0,48},{16,0},{32,16},{48,32},{64,112},{80,64},{96,80},{112,96},{1... | collective-permute-start | bytes 3145736 | tf_op jit(solution)/shard_map/ppermute | solution.py:253
  106.5 0.8 collective-permute-start.14
  107.4 3.0 %collective-permute-done.10.other_ref = f32[16,512,128]{2,1,0:T(8,128)S(1)} collective-permute-done((f32[16,512,128]{2,1,0:T(8,128)S(1)}, f32[16,512,128]{2,1,0:T(8,128)S(1)}, u32[]{:S(2)}, u32[]{:S(2)}) %collective-permute-start.10) | collective-permute-done | bytes 4194336 | tf_op jit(solution)/shard_map/ppermute | solution.py:266
  110.4 2.3 %split_amplitudes.1.rest_4_.rest_3_ = bf16[2,16,512,256]{3,2,1,0:T(8,128)(2,1)S(1)} custom-call(f32[16,512,128]{2,1,0:T(8,128)S(1)} %get-tuple-element.24.amp_ref, f32[16,512,128]{2,1,0:T(8,128)S(1)} %collective-permute-done.10.other_ref), custom_call_target="tpu_custom_call" | custom-call | flops 1048576 | bytes 25165824 | tf_op jit(solution)/shard_map/split_amplitudes/pallas_call | solution.py:180
  112.7 8.5 %product.3.refs_2_.rest_4_ = f32[512,2048]{1,0:T(8,128)S(1)} custom-call(s32[16,128]{1,0:T(8,128)S(1)} %copy-done.5, f32[16,128,128]{2,1,0:T(8,128)S(1)} %get-tuple-element.19.rest_0_, f32[16,128,128]{2,1,0:T(8,128)S(1)} %collective-permute-done.3.refs_0_.rest_1_, f32[16,128,128]{2,1,0:T(8,128)S(1)} %collective-permute-done.4.refs_1_.rest_2_, ...), custom_call_target="tpu_custom_call" | custom-call | flops 12884901888 | bytes 8388608 | tf_op jit(solution)/shard_map/product/pallas_call | solution.py:238
  121.1 8.9 %collective-permute-done.8.refs_0_.rest_0_ = f32[16,128,128]{2,1,0:T(8,128)S(1)} collective-permute-done((f32[16,128,128]{2,1,0:T(8,128)S(1)}, f32[16,128,128]{2,1,0:T(8,128)S(1)}, u32[]{:S(2)}, u32[]{:S(2)}) %collective-permute-start.8) | collective-permute-done | bytes 1048608 | tf_op jit(solution)/shard_map/ppermute | solution.py:253
  130.0 0.7 regroup.3
  130.8 3.2 %collective-permute-start.12 = (f32[5,128,128]{2,1,0:T(8,128)S(1)}, f32[5,128,128]{2,1,0:T(8,128)S(1)}, u32[]{:S(2)}, u32[]{:S(2)}) collective-permute-start(f32[5,128,128]{2,1,0:T(8,128)S(1)} %get-tuple-element.26), channel_id=1, source_target_pairs={{0,48},{16,0},{32,16},{48,32},{64,112},{80,64},{96,80},{112,96},{1... | collective-permute-start | bytes 983048 | tf_op jit(solution)/shard_map/ppermute | solution.py:253
  134.1 0.8 collective-permute-start.13
  134.9 6.6 %product.4.rest_4_ = f32[512,2048]{1,0:T(8,128)S(1)} custom-call(s32[16,128]{1,0:T(8,128)S(1)} %copy-done.5, f32[16,128,128]{2,1,0:T(8,128)S(1)} %collective-permute-done.8.refs_0_.rest_0_, f32[16,128,128]{2,1,0:T(8,128)S(1)} %collective-permute-done.9.refs_1_.rest_1_, f32[16,128,128]{2,1,0:T(8,128)S(1)} %collective-permute-done.14.rest_2_, ...), custom_call_target="tpu_custom_call" | custom-call | flops 9663676416 | bytes 8388608 | tf_op jit(solution)/shard_map/product/pallas_call | solution.py:238
  141.5 2.7 %collective-permute-done.13.rest_2_ = f32[6,128,128]{2,1,0:T(8,128)S(1)} collective-permute-done((f32[6,128,128]{2,1,0:T(8,128)S(1)}, f32[6,128,128]{2,1,0:T(8,128)S(1)}, u32[]{:S(2)}, u32[]{:S(2)}) %collective-permute-start.13) | collective-permute-done | bytes 393248 | tf_op jit(solution)/shard_map/ppermute | solution.py:257
  144.2 4.6 %product.5 = f32[512,2048]{1,0:T(8,128)} custom-call(s32[16,128]{1,0:T(8,128)S(1)} %copy-done.5, f32[5,128,128]{2,1,0:T(8,128)S(1)} %collective-permute-done.11.rest_0_, f32[5,128,128]{2,1,0:T(8,128)S(1)} %collective-permute-done.12.rest_1_, f32[6,128,128]{2,1,0:T(8,128)S(1)} %collective-permute-done.13.rest_2_, ...), custom_call_target="tpu_custom_call" | custom-call | flops 3221225472 | bytes 8388608 | tf_op jit(solution)/shard_map/product/pallas_call | solution.py:238
  (21 shorter events, 1.1 us)
Async XLA Ops:
  6.6 7.7 %copy-start = (f32[2,512,128]{2,1,0:T(8,128)S(1)}, f32[2,512,128]{2,1,0:T(8,128)}, u32[]{:S(2)}) copy-start(f32[2,512,128]{2,1,0:T(8,128)} %amp_ref.1) | copy-start | bytes 1572868
  6.6 57.6 %copy-start.5 = (s32[16,128]{1,0:T(8,128)S(1)}, s32[16,128]{1,0:T(8,128)}, u32[]{:S(2)}) copy-start(s32[16,128]{1,0:T(8,128)} %get-tuple-element.17.meta_ref) | copy-start | bytes 24580
  6.6 57.6 %all-to-all-start = ((f32[16,2,128,128]{3,2,1,0:T(8,128)}), f32[16,2,128,128]{3,2,1,0:T(8,128)S(1)}, u32[]{:S(2)}, u32[]{:S(2)}) async-start(f32[16,2,128,128]{3,2,1,0:T(8,128)} %get-tuple-element.18), calls=%async_computation | async-start | bytes 4194304 | tf_op jit(solution)/shard_map/all_to_all | solution.py:276
  14.3 38.7 %collective-permute-start.1 = (f32[2,512,128]{2,1,0:T(8,128)S(1)}, f32[2,512,128]{2,1,0:T(8,128)S(1)}, u32[]{:S(2)}, u32[]{:S(2)}) collective-permute-start(f32[2,512,128]{2,1,0:T(8,128)S(1)} %copy-done), channel_id=1, source_target_pairs={{0,4},{1,5},{2,6},{3,7},{4,8},{5,9},{6,10},{7,11},{8,12},{9,13},{1... | collective-permute-start | bytes 1572872 | tf_op jit(solution)/shard_map/ppermute | solution.py:262
  14.5 48.9 %collective-permute-start = (f32[2,512,128]{2,1,0:T(8,128)S(1)}, f32[2,512,128]{2,1,0:T(8,128)S(1)}, u32[]{:S(2)}, u32[]{:S(2)}) collective-permute-start(f32[2,512,128]{2,1,0:T(8,128)S(1)} %copy-done), channel_id=1, source_target_pairs={{0,2},{1,3},{2,0},{3,1},{4,6},{5,7},{6,4},{7,5},{8,10},{9,11},{10,... | collective-permute-start | bytes 1572872 | tf_op jit(solution)/shard_map/ppermute | solution.py:266
  17.9 46.3 %collective-permute-start.2 = (f32[2,512,128]{2,1,0:T(8,128)S(1)}, f32[2,512,128]{2,1,0:T(8,128)S(1)}, u32[]{:S(2)}, u32[]{:S(2)}) collective-permute-start(f32[2,512,128]{2,1,0:T(8,128)S(1)} %copy-done), channel_id=1, source_target_pairs={{0,10},{1,11},{2,8},{3,9},{4,14},{5,15},{6,12},{7,13},{8,2},{9,3},... | collective-permute-start | bytes 1572872 | tf_op jit(solution)/shard_map/ppermute | solution.py:275
  53.0 0.8 copy-start.1
  63.4 0.8 copy-start.3
  64.2 1.0 copy-start.2
  65.3 1.0 copy-start.4
  68.8 26.4 %collective-permute-start.6 = (f32[4,512,128]{2,1,0:T(8,128)S(1)}, f32[4,512,128]{2,1,0:T(8,128)S(1)}, u32[]{:S(2)}, u32[]{:S(2)}) collective-permute-start(f32[4,512,128]{2,1,0:T(8,128)S(1)} %get-tuple-element.20.refs_3_), channel_id=1, source_target_pairs={{0,12},{1,13},{2,14},{3,15},{4,0},{5,1},{6,2},{7,3},{8,4},{9,5},{1... | collective-permute-start | bytes 3145736 | tf_op jit(solution)/shard_map/ppermute | solution.py:262
  69.9 25.3 %collective-permute-start.7 = (f32[4,512,128]{2,1,0:T(8,128)S(1)}, f32[4,512,128]{2,1,0:T(8,128)S(1)}, u32[]{:S(2)}, u32[]{:S(2)}) collective-permute-start(f32[4,512,128]{2,1,0:T(8,128)S(1)} %get-tuple-element.21.refs_7_), channel_id=1, source_target_pairs={{0,4},{1,5},{2,6},{3,7},{4,8},{5,9},{6,10},{7,11},{8,12},{9,13},{1... | collective-permute-start | bytes 3145736 | tf_op jit(solution)/shard_map/ppermute | solution.py:262
  72.1 24.6 %collective-permute-start.5 = (f32[16,128,128]{2,1,0:T(8,128)S(1)}, f32[16,128,128]{2,1,0:T(8,128)S(1)}, u32[]{:S(2)}, u32[]{:S(2)}) collective-permute-start(f32[16,128,128]{2,1,0:T(8,128)S(1)} %get-tuple-element.19.rest_0_), channel_id=1, source_target_pairs={{0,64},{16,80},{32,96},{48,112},{64,0},{80,16},{96,32},{112,48},{1... | collective-permute-start | bytes 3145736 | tf_op jit(solution)/shard_map/ppermute | solution.py:257
  73.3 25.8 %collective-permute-start.4 = (f32[16,128,128]{2,1,0:T(8,128)S(1)}, f32[16,128,128]{2,1,0:T(8,128)S(1)}, u32[]{:S(2)}, u32[]{:S(2)}) collective-permute-start(f32[16,128,128]{2,1,0:T(8,128)S(1)} %get-tuple-element.19.rest_0_), channel_id=1, source_target_pairs={{0,48},{16,0},{32,16},{48,32},{64,112},{80,64},{96,80},{112,96},{1... | collective-permute-start | bytes 3145736 | tf_op jit(solution)/shard_map/ppermute | solution.py:253
  77.3 25.2 %collective-permute-start.3 = (f32[16,128,128]{2,1,0:T(8,128)S(1)}, f32[16,128,128]{2,1,0:T(8,128)S(1)}, u32[]{:S(2)}, u32[]{:S(2)}) collective-permute-start(f32[16,128,128]{2,1,0:T(8,128)S(1)} %get-tuple-element.19.rest_0_), channel_id=1, source_target_pairs={{0,16},{16,32},{32,48},{48,0},{64,80},{80,96},{96,112},{112,64},{1... | collective-permute-start | bytes 3145736 | tf_op jit(solution)/shard_map/ppermute | solution.py:253
  103.1 7.2 %collective-permute-start.10 = (f32[16,512,128]{2,1,0:T(8,128)S(1)}, f32[16,512,128]{2,1,0:T(8,128)S(1)}, u32[]{:S(2)}, u32[]{:S(2)}) collective-permute-start(f32[16,512,128]{2,1,0:T(8,128)S(1)} %get-tuple-element.24.amp_ref), channel_id=1, source_target_pairs={{0,1},{1,0},{2,3},{3,2},{4,5},{5,4},{6,7},{7,6},{8,9},{9,8},{10,11... | collective-permute-start | bytes 12582920 | tf_op jit(solution)/shard_map/ppermute | solution.py:266
  103.2 26.8 %collective-permute-start.8 = (f32[16,128,128]{2,1,0:T(8,128)S(1)}, f32[16,128,128]{2,1,0:T(8,128)S(1)}, u32[]{:S(2)}, u32[]{:S(2)}) collective-permute-start(f32[16,128,128]{2,1,0:T(8,128)S(1)} %get-tuple-element.22), channel_id=1, source_target_pairs={{0,16},{16,32},{32,48},{48,0},{64,80},{80,96},{96,112},{112,64},{1... | collective-permute-start | bytes 3145736 | tf_op jit(solution)/shard_map/ppermute | solution.py:253
  103.3 26.7 %collective-permute-start.9 = (f32[16,128,128]{2,1,0:T(8,128)S(1)}, f32[16,128,128]{2,1,0:T(8,128)S(1)}, u32[]{:S(2)}, u32[]{:S(2)}) collective-permute-start(f32[16,128,128]{2,1,0:T(8,128)S(1)} %get-tuple-element.23), channel_id=1, source_target_pairs={{0,48},{16,0},{32,16},{48,32},{64,112},{80,64},{96,80},{112,96},{1... | collective-permute-start | bytes 3145736 | tf_op jit(solution)/shard_map/ppermute | solution.py:253
  106.5 28.4 %collective-permute-start.14 = (f32[16,128,128]{2,1,0:T(8,128)S(1)}, f32[16,128,128]{2,1,0:T(8,128)S(1)}, u32[]{:S(2)}, u32[]{:S(2)}) collective-permute-start(f32[16,128,128]{2,1,0:T(8,128)S(1)} %get-tuple-element.28), channel_id=1, source_target_pairs={{0,64},{16,80},{32,96},{48,112},{64,0},{80,16},{96,32},{112,48},{1... | collective-permute-start | bytes 3145736 | tf_op jit(solution)/shard_map/ppermute | solution.py:257
  130.8 10.7 %collective-permute-start.11 = (f32[5,128,128]{2,1,0:T(8,128)S(1)}, f32[5,128,128]{2,1,0:T(8,128)S(1)}, u32[]{:S(2)}, u32[]{:S(2)}) collective-permute-start(f32[5,128,128]{2,1,0:T(8,128)S(1)} %get-tuple-element.25), channel_id=1, source_target_pairs={{0,16},{16,32},{32,48},{48,0},{64,80},{80,96},{96,112},{112,64},{1... | collective-permute-start | bytes 983048 | tf_op jit(solution)/shard_map/ppermute | solution.py:253
  130.8 10.6 %collective-permute-start.12 = (f32[5,128,128]{2,1,0:T(8,128)S(1)}, f32[5,128,128]{2,1,0:T(8,128)S(1)}, u32[]{:S(2)}, u32[]{:S(2)}) collective-permute-start(f32[5,128,128]{2,1,0:T(8,128)S(1)} %get-tuple-element.26), channel_id=1, source_target_pairs={{0,48},{16,0},{32,16},{48,32},{64,112},{80,64},{96,80},{112,96},{1... | collective-permute-start | bytes 983048 | tf_op jit(solution)/shard_map/ppermute | solution.py:253
  134.1 10.1 %collective-permute-start.13 = (f32[6,128,128]{2,1,0:T(8,128)S(1)}, f32[6,128,128]{2,1,0:T(8,128)S(1)}, u32[]{:S(2)}, u32[]{:S(2)}) collective-permute-start(f32[6,128,128]{2,1,0:T(8,128)S(1)} %get-tuple-element.27), channel_id=1, source_target_pairs={{0,64},{16,80},{32,96},{48,112},{64,0},{80,16},{96,32},{112,48},{1... | collective-permute-start | bytes 1179656 | tf_op jit(solution)/shard_map/ppermute | solution.py:257

commit v3 on v2

--- a/solution.py
+++ b/solution.py
@@ -97,7 +97,7 @@
     )(readers, rows, columns, tiles)
 
 
-def compact_kernel(meta_ref, arrived_ref, amp_ref, side_ref, left_ref, far_ref, out_ref, minus_ref, plus_ref, sems):
+def compact_kernel(meta_ref, arrived_ref, amp_ref, side_ref, left_ref, out_ref, minus_ref, plus_ref, sems):
     me_row = lax.axis_index("row")
     copies = []
 
@@ -117,19 +117,19 @@
         one.wait()
 
 
-def compact(meta, arrived, amplitudes, side, amp_left, side_far):
+def compact(meta, arrived, amplitudes, side, amp_left):
     tiles = STEPS * CHUNK
     hbm, vmem = pl.BlockSpec(memory_space=pltpu.HBM), pl.BlockSpec(memory_space=pltpu.VMEM)
     pair = jax.ShapeDtypeStruct((2 * STEPS,) + amplitudes.shape[1:], jnp.float32)
     return pl.pallas_call(
         compact_kernel,
         out_shape=[jax.ShapeDtypeStruct((tiles, TILE, TILE), jnp.float32), pair, pair],
-        in_specs=[pl.BlockSpec(memory_space=pltpu.SMEM)] + [hbm] * 5,
+        in_specs=[pl.BlockSpec(memory_space=pltpu.SMEM)] + [hbm] * 4,
         out_specs=[vmem] * 3,
         scratch_shapes=[pltpu.SemaphoreType.DMA((tiles + 4,))],
         compiler_params=pltpu.CompilerParams(vmem_limit_bytes=SMALL_LIMIT),
         name="compact",
-    )(meta, arrived, amplitudes, side, amp_left, side_far)
+    )(meta, arrived, amplitudes, side, amp_left)
 
 
 def regroup_kernel(plan, *refs):
@@ -165,28 +165,33 @@
     )(*chunks, *earlier)
 
 
-def split_kernel(amp_ref, other_ref, out_ref):
-    for core, ref in enumerate((amp_ref, other_ref)):
-        for n in range(ref.shape[0]):
-            value = ref[n]
-            high = value.astype(jnp.bfloat16)
-            out_ref[core, n, :, :TILE] = high
-            out_ref[core, n, :, TILE:] = (value - high.astype(jnp.float32)).astype(jnp.bfloat16)
+def split_kernel(*refs):
+    out_ref = refs[-1]
+    count = len(refs) // 2
+    for core in range(2):
+        at = 0
+        for ref in refs[core * count : (core + 1) * count]:
+            for n in range(ref.shape[0]):
+                value = ref[n]
+                high = value.astype(jnp.bfloat16)
+                out_ref[core, at, :, :TILE] = high
+                out_ref[core, at, :, TILE:] = (value - high.astype(jnp.float32)).astype(jnp.bfloat16)
+                at += 1
 
 
 def split_amplitudes(ours, others):
-    count, rows = ours.shape[:2]
-    block = pl.BlockSpec((2, rows, TILE), lambda n: (n, 0, 0))
+    count, rows = sum(p.shape[0] for p in ours), ours[0].shape[1]
+    blocks = [pl.BlockSpec((p.shape[0], rows // 8, TILE), lambda n: (0, n, 0)) for p in ours]
     return pl.pallas_call(
         split_kernel,
         out_shape=jax.ShapeDtypeStruct((2, count, rows, 2 * TILE), jnp.bfloat16),
-        grid=(count // 2,),
-        in_specs=[block, block],
-        out_specs=pl.BlockSpec((2, 2, rows, 2 * TILE), lambda n: (0, n, 0, 0)),
+        grid=(8,),
+        in_specs=blocks * 2,
+        out_specs=pl.BlockSpec((2, count, rows // 8, 2 * TILE), lambda n: (0, 0, n, 0)),
         compiler_params=pltpu.CompilerParams(vmem_limit_bytes=SMALL_LIMIT),
-        cost_estimate=pl.CostEstimate(flops=2**20, bytes_accessed=24 * 2**20, transcendentals=0),
+        cost_estimate=pl.CostEstimate(flops=2**20, bytes_accessed=2**20, transcendentals=0),
         name="split_amplitudes",
-    )(ours, others)
+    )(*ours, *others)
 
 
 def product_kernel(places, has_start, meta_ref, *rest):
@@ -210,7 +215,8 @@
                 s = number // CHUNK
                 code = meta_ref[s * 8, (number % CHUNK) * N_ROW + source]
                 column = code // NT_DEV
-                away = ((column // 4 + 4 - me_col // 4) % 4) * 2 + ((column ^ me_col) // 2) % 2
+                steps = (column // 4 + 4 - me_col // 4) % 4
+                away = (steps ^ (steps // 2)) * 2 + ((column ^ me_col) // 2) % 2
                 tile = ref[at + m]
                 high = tile.astype(jnp.bfloat16)
                 low = (tile - high.astype(jnp.float32)).astype(jnp.bfloat16)
@@ -242,7 +248,7 @@
         out_specs=vmem,
         compiler_params=pltpu.CompilerParams(vmem_limit_bytes=VMEM_LIMIT),
         cost_estimate=pl.CostEstimate(
-            flops=6 * tiles * rows * 4 * TILE * TILE, bytes_accessed=8 * 2**20, transcendentals=0
+            flops=tiles * rows * TILE, bytes_accessed=2**20, transcendentals=0
         ),
         name="product",
     )(meta, *operands)
@@ -272,30 +278,29 @@
         tile_reader.reshape(held), tile_rows.reshape(held), tile_column.reshape(held), integrals
     )
     side, amp_left = flip(amplitudes, 2), along_x(amplitudes, 1)
-    side_far = lax.ppermute(amplitudes, "col", [(c, (c ^ 2) ^ 8) for c in range(N_COL)])
     arrived = lax.all_to_all(sent, "col", split_axis=0, concat_axis=0, tiled=True)
-    own, minus, plus = compact(meta, arrived, amplitudes, side, amp_left, side_far)
+    own, minus, plus = compact(meta, arrived, amplitudes, side, amp_left)
 
     left, right, other = along_z(own, 1), along_z(own, -1), across_y(own)
     from_right, from_left = along_x(minus, -1), along_x(plus, 1)
 
-    up, down, across, ours = regroup(
-        [left, right, other, minus, from_right, from_left, side_far, plus],
+    up, down, across, side_far, ours = regroup(
+        [left, right, other, minus, from_right, from_left, plus],
         [
             [(0, 0, 8), (2, 0, 8)],
             [(1, 8, 8), (2, 8, 8)],
             [(0, 8, 8), (1, 0, 8)],
-            [(3, 0, 4), (4, 0, 4), (5, 0, 2), (6, 0, 2), (7, 0, 2), (5, 2, 2)],
+            [(4, 2, 2)],
+            [(3, 0, 4), (4, 0, 4), (6, 0, 2), (5, 2, 2), (5, 0, 2)],
         ],
     )
     up, down, across = along_z(up, 1), along_z(down, -1), across_y(across)
-    amps = split_amplitudes(ours, flip(ours, 1))
+    ours = [ours, along_x(side_far, -1)]
+    amps = split_amplitudes(ours, [flip(p, 1) for p in ours])
     places = [[(dy, dz, 0, 16)] for dy, dz in ((0, 0), (0, 3), (0, 1), (1, 0))]
     ladder = product(meta, [own, left, right, other], places, amps)
 
-    far_up, far_down, far_across = regroup(
-        [up, down], [[(0, 8, 5)], [(1, 11, 5)], [(0, 5, 3), (1, 0, 3)]], ladder
-    )
+    far_up, far_down, far_across = regroup([up, down], [[(0, 8, 5)], [(1, 11, 5)], [(0, 5, 3), (1, 0, 3)]], ladder)
     far_up, far_down, far_across = along_z(far_up, 1), along_z(far_down, -1), across_y(far_across)
     places = [
         [(0, 2, 0, 8), (1, 3, 0, 8)],

time: 150 us -> 137 us (0.913)
  waiting for transfers between devices: 82.1 us -> 73.6 us
  starting transfers between devices: 30.5 us -> 28.2 us
  local copies, waits for them, and re-layouts: 5.01 us -> 3.16 us
    ppermute x2 -> x3, waiting for transfers between devices: 12.5 us -> 36.2 us  [flip(): return lax.ppermute(value, 'col', [(c, c ^ bit) for c in range(N_COL)])]
    ppermute x3 -> x4, waiting for transfers between devices: 50.7 us -> 29.2 us  [along_x(): return lax.ppermute(value, 'col', pairs)]
    ppermute x6, waiting for transfers between devices: 14.7 us -> 6.78 us  [along_z(): return lax.ppermute(value, 'row', pairs)]
    ppermute x3, waiting for transfers between devices: 4.14 us -> 1.47 us  [across_y(): return lax.ppermute(value, 'row', [(i, i ^ Z) for i in range(N_ROW)])]
    ppermute x1 -> x0, starting transfers between devices: 2.36 us -> none  [shards(): lax.ppermute(amplitudes, 'col', [(c, c ^ 2 ^ 8) for c in range(N_COL)])]
    unnamed x12 -> x8, local copies, waits for them, and re-layouts: 3.71 us -> 1.85 us
    ppermute x3 -> x4, starting transfers between devices: 3.47 us -> 3.94 us  [along_x(): return lax.ppermute(value, 'col', pairs)]
    ppermute x2 -> x3, starting transfers between devices: 3.51 us -> 3.14 us  [flip(): return lax.ppermute(value, 'col', [(c, c ^ bit) for c in range(N_COL)])]
  transfers between devices with their start and end apart: 16 -> 17, of which waited for: 9 -> 9; matrix products, arithmetic and copies ran while one was open for 0% -> 0% of each run, Pallas kernels for 12% -> 13%
where the time goes in v3:
time: 137 us
  waiting for transfers between devices  73.6 us (54%)
  Pallas kernels  31.5 us (23%)
  starting transfers between devices  28.2 us (21%)
  local copies, waits for them, and re-layouts  3.16 us (2%)
    ppermute x3, waiting for transfers between devices, flip(): return lax.ppermute(value, 'col', [(c, c ^ bit) for c in range(N_COL)])  36.2 us
    ppermute x4, waiting for transfers between devices, along_x(): return lax.ppermute(value, 'col', pairs)  29.2 us
    pallas_call x3, Pallas kernels, product(): pl.pallas_call(functools.partial(product_kernel, places, start is not Non...  19.7 us
    ppermute x6, starting transfers between devices, along_z(): return lax.ppermute(value, 'row', pairs)  10.5 us
    all_to_all x1, starting transfers between devices, shards(): lax.all_to_all(sent, 'col', split_axis=0, concat_axis=0, tiled=True)  7.6 us
    ppermute x6, waiting for transfers between devices, along_z(): return lax.ppermute(value, 'row', pairs)  6.78 us
    pallas_call x1, Pallas kernels, route(): pl.pallas_call(route_kernel, out_shape=(jax.ShapeDtypeStruct((8 * STEPS,...  5.29 us
    ppermute x4, starting transfers between devices, along_x(): return lax.ppermute(value, 'col', pairs)  3.94 us
  transfers between devices with their start and end apart: 17, of which 9 were waited for; matrix products, arithmetic and copies ran while one was open for 0% of the time, Pallas kernels for 13%

profile of v3, /device:TPU:6, one launch (start us, length us, event | category | flops | bytes accessed | tf_op | source)
XLA Modules:
  0.0 136.6 jit_solution(8273462375391853004)
XLA Ops:
  0.0 1.3 copy_bitcast_fusion
  1.3 5.3 %route.1 = (s32[16,128]{1,0:T(8,128)}, f32[16,2,128,128]{3,2,1,0:T(8,128)}) custom-call(s32[2,8,128]{2,1,0:T(8,128)} %bitcast.7, s32[2,8,128]{2,1,0:T(8,128)} %get-tuple-element.32.row_ref, s32[2,8,128]{2,1,0:T(8,128)} %get-tuple-element.31.column_ref, f32[2,64,128,128]{3,2,1,0:T(8,128)} %tiles_ref.1), custom_call_target="tpu_custom_call" | custom-call | tf_op jit(solution)/shard_map/route/pallas_call | solution.py:83
  6.6 7.6 %all-to-all-start = ((f32[16,2,128,128]{3,2,1,0:T(8,128)}), f32[16,2,128,128]{3,2,1,0:T(8,128)S(1)}, u32[]{:S(2)}, u32[]{:S(2)}) async-start(f32[16,2,128,128]{3,2,1,0:T(8,128)} %get-tuple-element.19), calls=%async_computation | async-start | bytes 4194304 | tf_op jit(solution)/shard_map/all_to_all | solution.py:281
  14.2 3.0 %collective-permute-start = (f32[2,512,128]{2,1,0:T(8,128)S(1)}, f32[2,512,128]{2,1,0:T(8,128)S(1)}, u32[]{:S(2)}, u32[]{:S(2)}) collective-permute-start(f32[2,512,128]{2,1,0:T(8,128)S(1)} %copy-done), channel_id=1, source_target_pairs={{0,2},{1,3},{2,0},{3,1},{4,6},{5,7},{6,4},{7,5},{8,10},{9,11},{10,... | collective-permute-start | bytes 1572872 | tf_op jit(solution)/shard_map/ppermute | solution.py:272
  17.3 0.6 collective-permute-start.1
  17.9 34.3 %collective-permute-done.side_ref = f32[2,512,128]{2,1,0:T(8,128)S(1)} collective-permute-done((f32[2,512,128]{2,1,0:T(8,128)S(1)}, f32[2,512,128]{2,1,0:T(8,128)S(1)}, u32[]{:S(2)}, u32[]{:S(2)}) %collective-permute-start) | collective-permute-done | bytes 524320 | tf_op jit(solution)/shard_map/ppermute | solution.py:272
  52.1 0.4 collective-permute-done.1.left_ref
  52.5 0.8 copy-done.1
  53.3 1.0 copy-done.2
  54.4 2.5 %compact.1 = (f32[16,128,128]{2,1,0:T(8,128)S(1)}, f32[4,512,128]{2,1,0:T(8,128)S(1)}, f32[4,512,128]{2,1,0:T(8,128)S(1)}) custom-call(s32[16,128]{1,0:T(8,128)S(1)} %copy-done.3, f32[16,2,128,128]{3,2,1,0:T(8,128)S(1)} %all-to-all-done.arrived_ref, f32[2,512,128]{2,1,0:T(8,128)S(1)} %copy-done, f32[2,512,128]{2,1,0:T(8,128)S(1)} %collective-permute-done.side_ref, ...), custom_call_target="tpu_custom_call" | custom-call | tf_op jit(solution)/shard_map/compact/pallas_call | solution.py:124
  56.8 0.5 collective-permute-start.5
  57.4 2.8 %collective-permute-start.6 = (f32[4,512,128]{2,1,0:T(8,128)S(1)}, f32[4,512,128]{2,1,0:T(8,128)S(1)}, u32[]{:S(2)}, u32[]{:S(2)}) collective-permute-start(f32[4,512,128]{2,1,0:T(8,128)S(1)} %get-tuple-element.22.refs_6_), channel_id=1, source_target_pairs={{0,4},{1,5},{2,6},{3,7},{4,8},{5,9},{6,10},{7,11},{8,12},{9,13},{1... | collective-permute-start | bytes 3145736 | tf_op jit(solution)/shard_map/ppermute | solution.py:268
  60.2 1.2 collective-permute-start.4
  61.4 4.0 %collective-permute-start.3 = (f32[16,128,128]{2,1,0:T(8,128)S(1)}, f32[16,128,128]{2,1,0:T(8,128)S(1)}, u32[]{:S(2)}, u32[]{:S(2)}) collective-permute-start(f32[16,128,128]{2,1,0:T(8,128)S(1)} %get-tuple-element.20.rest_0_), channel_id=1, source_target_pairs={{0,48},{16,0},{32,16},{48,32},{64,112},{80,64},{96,80},{112,96},{1... | collective-permute-start | bytes 3145736 | tf_op jit(solution)/shard_map/ppermute | solution.py:259
  65.4 17.5 %collective-permute-done.5.refs_4_ = f32[4,512,128]{2,1,0:T(8,128)S(1)} collective-permute-done((f32[4,512,128]{2,1,0:T(8,128)S(1)}, f32[4,512,128]{2,1,0:T(8,128)S(1)}, u32[]{:S(2)}, u32[]{:S(2)}) %collective-permute-start.5) | collective-permute-done | bytes 1048608 | tf_op jit(solution)/shard_map/ppermute | solution.py:268
  82.9 1.5 %collective-permute-done.4.refs_2_.rest_3_ = f32[16,128,128]{2,1,0:T(8,128)S(1)} collective-permute-done((f32[16,128,128]{2,1,0:T(8,128)S(1)}, f32[16,128,128]{2,1,0:T(8,128)S(1)}, u32[]{:S(2)}, u32[]{:S(2)}) %collective-permute-start.4) | collective-permute-done | bytes 1048608 | tf_op jit(solution)/shard_map/ppermute | solution.py:263
  84.3 2.5 %collective-permute-done.3.refs_1_.rest_2_ = f32[16,128,128]{2,1,0:T(8,128)S(1)} collective-permute-done((f32[16,128,128]{2,1,0:T(8,128)S(1)}, f32[16,128,128]{2,1,0:T(8,128)S(1)}, u32[]{:S(2)}, u32[]{:S(2)}) %collective-permute-start.3) | collective-permute-done | bytes 1048608 | tf_op jit(solution)/shard_map/ppermute | solution.py:259
  86.8 3.4 %collective-permute-done.2.refs_0_.rest_1_ = f32[16,128,128]{2,1,0:T(8,128)S(1)} collective-permute-done((f32[16,128,128]{2,1,0:T(8,128)S(1)}, f32[16,128,128]{2,1,0:T(8,128)S(1)}, u32[]{:S(2)}, u32[]{:S(2)}) %collective-permute-start.2) | collective-permute-done | bytes 1048608 | tf_op jit(solution)/shard_map/ppermute | solution.py:259
  90.2 0.6 regroup.2
  90.9 0.1 collective-permute-start.10
  91.1 3.2 %collective-permute-start.8 = (f32[16,128,128]{2,1,0:T(8,128)S(1)}, f32[16,128,128]{2,1,0:T(8,128)S(1)}, u32[]{:S(2)}, u32[]{:S(2)}) collective-permute-start(f32[16,128,128]{2,1,0:T(8,128)S(1)} %get-tuple-element.24), channel_id=1, source_target_pairs={{0,48},{16,0},{32,16},{48,32},{64,112},{80,64},{96,80},{112,96},{1... | collective-permute-start | bytes 3145736 | tf_op jit(solution)/shard_map/ppermute | solution.py:259
  94.3 0.8 collective-permute-start.15
  95.2 11.3 %collective-permute-done.9.refs_1_ = f32[2,512,128]{2,1,0:T(8,128)S(1)} collective-permute-done((f32[2,512,128]{2,1,0:T(8,128)S(1)}, f32[2,512,128]{2,1,0:T(8,128)S(1)}, u32[]{:S(2)}, u32[]{:S(2)}) %collective-permute-start.9) | collective-permute-done | bytes 524320 | tf_op jit(solution)/shard_map/ppermute | solution.py:268
  106.5 1.9 %collective-permute-done.11.refs_3_ = f32[2,512,128]{2,1,0:T(8,128)S(1)} collective-permute-done((f32[2,512,128]{2,1,0:T(8,128)S(1)}, f32[2,512,128]{2,1,0:T(8,128)S(1)}, u32[]{:S(2)}, u32[]{:S(2)}) %collective-permute-start.11) | collective-permute-done | bytes 524320 | tf_op jit(solution)/shard_map/ppermute | solution.py:272
  108.4 2.7 %split_amplitudes.1.rest_4_.rest_3_ = bf16[2,16,512,256]{3,2,1,0:T(8,128)(2,1)S(1)} custom-call(f32[14,512,128]{2,1,0:T(8,128)S(1)} %get-tuple-element.25.refs_0_, f32[2,512,128]{2,1,0:T(8,128)S(1)} %collective-permute-done.9.refs_1_, f32[14,512,128]{2,1,0:T(8,128)S(1)} %collective-permute-done.10.refs_2_, f32[2,512,128]{2,1,0:T(8,128)S(1)} %collective-permute-done.11.refs_3_), custom_call_target="tpu_custom_call" | custom-call | flops 1048576 | bytes 1048576 | tf_op jit(solution)/shard_map/split_amplitudes/pallas_call | solution.py:185
  111.1 8.5 %product.3.refs_2_.rest_4_ = f32[512,2048]{1,0:T(8,128)S(1)} custom-call(s32[16,128]{1,0:T(8,128)S(1)} %copy-done.3, f32[16,128,128]{2,1,0:T(8,128)S(1)} %get-tuple-element.20.rest_0_, f32[16,128,128]{2,1,0:T(8,128)S(1)} %collective-permute-done.2.refs_0_.rest_1_, f32[16,128,128]{2,1,0:T(8,128)S(1)} %collective-permute-done.3.refs_1_.rest_2_, ...), custom_call_target="tpu_custom_call" | custom-call | flops 4194304 | bytes 1048576 | tf_op jit(solution)/shard_map/product/pallas_call | solution.py:244
  119.6 0.8 regroup.3
  120.3 0.9 collective-permute-start.14
  121.2 3.2 %collective-permute-start.13 = (f32[5,128,128]{2,1,0:T(8,128)S(1)}, f32[5,128,128]{2,1,0:T(8,128)S(1)}, u32[]{:S(2)}, u32[]{:S(2)}) collective-permute-start(f32[5,128,128]{2,1,0:T(8,128)S(1)} %get-tuple-element.28), channel_id=1, source_target_pairs={{0,48},{16,0},{32,16},{48,32},{64,112},{80,64},{96,80},{112,96},{1... | collective-permute-start | bytes 983048 | tf_op jit(solution)/shard_map/ppermute | solution.py:259
  124.5 6.6 %product.4.rest_4_ = f32[512,2048]{1,0:T(8,128)S(1)} custom-call(s32[16,128]{1,0:T(8,128)S(1)} %copy-done.3, f32[16,128,128]{2,1,0:T(8,128)S(1)} %collective-permute-done.7.refs_0_.rest_0_, f32[16,128,128]{2,1,0:T(8,128)S(1)} %collective-permute-done.8.refs_1_.rest_1_, f32[16,128,128]{2,1,0:T(8,128)S(1)} %collective-permute-done.15.rest_2_, ...), custom_call_target="tpu_custom_call" | custom-call | flops 3145728 | bytes 1048576 | tf_op jit(solution)/shard_map/product/pallas_call | solution.py:244
  131.0 0.9 collective-permute-done.12.rest_0_
  131.9 4.6 %product.5 = f32[512,2048]{1,0:T(8,128)} custom-call(s32[16,128]{1,0:T(8,128)S(1)} %copy-done.3, f32[5,128,128]{2,1,0:T(8,128)S(1)} %collective-permute-done.12.rest_0_, f32[5,128,128]{2,1,0:T(8,128)S(1)} %collective-permute-done.13.rest_1_, f32[6,128,128]{2,1,0:T(8,128)S(1)} %collective-permute-done.14.rest_2_, ...), custom_call_target="tpu_custom_call" | custom-call | flops 1048576 | bytes 1048576 | tf_op jit(solution)/shard_map/product/pallas_call | solution.py:244
  (19 shorter events, 0.2 us)
Async XLA Ops:
  6.6 7.6 %copy-start = (f32[2,512,128]{2,1,0:T(8,128)S(1)}, f32[2,512,128]{2,1,0:T(8,128)}, u32[]{:S(2)}) copy-start(f32[2,512,128]{2,1,0:T(8,128)} %amp_ref.1) | copy-start | bytes 1572868
  6.6 46.7 %copy-start.3 = (s32[16,128]{1,0:T(8,128)S(1)}, s32[16,128]{1,0:T(8,128)}, u32[]{:S(2)}) copy-start(s32[16,128]{1,0:T(8,128)} %get-tuple-element.18.meta_ref) | copy-start | bytes 24580
  6.6 46.7 %all-to-all-start = ((f32[16,2,128,128]{3,2,1,0:T(8,128)}), f32[16,2,128,128]{3,2,1,0:T(8,128)S(1)}, u32[]{:S(2)}, u32[]{:S(2)}) async-start(f32[16,2,128,128]{3,2,1,0:T(8,128)} %get-tuple-element.19), calls=%async_computation | async-start | bytes 4194304 | tf_op jit(solution)/shard_map/all_to_all | solution.py:281
  14.2 37.9 %collective-permute-start = (f32[2,512,128]{2,1,0:T(8,128)S(1)}, f32[2,512,128]{2,1,0:T(8,128)S(1)}, u32[]{:S(2)}, u32[]{:S(2)}) collective-permute-start(f32[2,512,128]{2,1,0:T(8,128)S(1)} %copy-done), channel_id=1, source_target_pairs={{0,2},{1,3},{2,0},{3,1},{4,6},{5,7},{6,4},{7,5},{8,10},{9,11},{10,... | collective-permute-start | bytes 1572872 | tf_op jit(solution)/shard_map/ppermute | solution.py:272
  17.3 35.2 %collective-permute-start.1 = (f32[2,512,128]{2,1,0:T(8,128)S(1)}, f32[2,512,128]{2,1,0:T(8,128)S(1)}, u32[]{:S(2)}, u32[]{:S(2)}) collective-permute-start(f32[2,512,128]{2,1,0:T(8,128)S(1)} %copy-done), channel_id=1, source_target_pairs={{0,4},{1,5},{2,6},{3,7},{4,8},{5,9},{6,10},{7,11},{8,12},{9,13},{1... | collective-permute-start | bytes 1572872 | tf_op jit(solution)/shard_map/ppermute | solution.py:268
  52.5 0.8 copy-start.1
  53.3 1.0 copy-start.2
  56.8 26.0 %collective-permute-start.5 = (f32[4,512,128]{2,1,0:T(8,128)S(1)}, f32[4,512,128]{2,1,0:T(8,128)S(1)}, u32[]{:S(2)}, u32[]{:S(2)}) collective-permute-start(f32[4,512,128]{2,1,0:T(8,128)S(1)} %get-tuple-element.21.refs_3_), channel_id=1, source_target_pairs={{0,12},{1,13},{2,14},{3,15},{4,0},{5,1},{6,2},{7,3},{8,4},{9,5},{1... | collective-permute-start | bytes 3145736 | tf_op jit(solution)/shard_map/ppermute | solution.py:268
  57.4 25.5 %collective-permute-start.6 = (f32[4,512,128]{2,1,0:T(8,128)S(1)}, f32[4,512,128]{2,1,0:T(8,128)S(1)}, u32[]{:S(2)}, u32[]{:S(2)}) collective-permute-start(f32[4,512,128]{2,1,0:T(8,128)S(1)} %get-tuple-element.22.refs_6_), channel_id=1, source_target_pairs={{0,4},{1,5},{2,6},{3,7},{4,8},{5,9},{6,10},{7,11},{8,12},{9,13},{1... | collective-permute-start | bytes 3145736 | tf_op jit(solution)/shard_map/ppermute | solution.py:268
  60.2 24.2 %collective-permute-start.4 = (f32[16,128,128]{2,1,0:T(8,128)S(1)}, f32[16,128,128]{2,1,0:T(8,128)S(1)}, u32[]{:S(2)}, u32[]{:S(2)}) collective-permute-start(f32[16,128,128]{2,1,0:T(8,128)S(1)} %get-tuple-element.20.rest_0_), channel_id=1, source_target_pairs={{0,64},{16,80},{32,96},{48,112},{64,0},{80,16},{96,32},{112,48},{1... | collective-permute-start | bytes 3145736 | tf_op jit(solution)/shard_map/ppermute | solution.py:263
  61.4 25.4 %collective-permute-start.3 = (f32[16,128,128]{2,1,0:T(8,128)S(1)}, f32[16,128,128]{2,1,0:T(8,128)S(1)}, u32[]{:S(2)}, u32[]{:S(2)}) collective-permute-start(f32[16,128,128]{2,1,0:T(8,128)S(1)} %get-tuple-element.20.rest_0_), channel_id=1, source_target_pairs={{0,48},{16,0},{32,16},{48,32},{64,112},{80,64},{96,80},{112,96},{1... | collective-permute-start | bytes 3145736 | tf_op jit(solution)/shard_map/ppermute | solution.py:259
  65.4 24.8 %collective-permute-start.2 = (f32[16,128,128]{2,1,0:T(8,128)S(1)}, f32[16,128,128]{2,1,0:T(8,128)S(1)}, u32[]{:S(2)}, u32[]{:S(2)}) collective-permute-start(f32[16,128,128]{2,1,0:T(8,128)S(1)} %get-tuple-element.20.rest_0_), channel_id=1, source_target_pairs={{0,16},{16,32},{32,48},{48,0},{64,80},{80,96},{96,112},{112,64},{1... | collective-permute-start | bytes 3145736 | tf_op jit(solution)/shard_map/ppermute | solution.py:259
  90.9 17.6 %collective-permute-start.10 = (f32[14,512,128]{2,1,0:T(8,128)S(1)}, f32[14,512,128]{2,1,0:T(8,128)S(1)}, u32[]{:S(2)}, u32[]{:S(2)}) collective-permute-start(f32[14,512,128]{2,1,0:T(8,128)S(1)} %get-tuple-element.25.refs_0_), channel_id=1, source_target_pairs={{0,1},{1,0},{2,3},{3,2},{4,5},{5,4},{6,7},{7,6},{8,9},{9,8},{10,11... | collective-permute-start | bytes 11010056 | tf_op jit(solution)/shard_map/ppermute | solution.py:272
  90.9 15.6 %collective-permute-start.9 = (f32[2,512,128]{2,1,0:T(8,128)S(1)}, f32[2,512,128]{2,1,0:T(8,128)S(1)}, u32[]{:S(2)}, u32[]{:S(2)}) collective-permute-start(f32[2,512,128]{2,1,0:T(8,128)S(1)} %get-tuple-element.26), channel_id=1, source_target_pairs={{0,12},{1,13},{2,14},{3,15},{4,0},{5,1},{6,2},{7,3},{8,4},{9,5},{1... | collective-permute-start | bytes 1572872 | tf_op jit(solution)/shard_map/ppermute | solution.py:268
  91.0 28.5 %collective-permute-start.7 = (f32[16,128,128]{2,1,0:T(8,128)S(1)}, f32[16,128,128]{2,1,0:T(8,128)S(1)}, u32[]{:S(2)}, u32[]{:S(2)}) collective-permute-start(f32[16,128,128]{2,1,0:T(8,128)S(1)} %get-tuple-element.23), channel_id=1, source_target_pairs={{0,16},{16,32},{32,48},{48,0},{64,80},{80,96},{96,112},{112,64},{1... | collective-permute-start | bytes 3145736 | tf_op jit(solution)/shard_map/ppermute | solution.py:259
  91.1 28.4 %collective-permute-start.8 = (f32[16,128,128]{2,1,0:T(8,128)S(1)}, f32[16,128,128]{2,1,0:T(8,128)S(1)}, u32[]{:S(2)}, u32[]{:S(2)}) collective-permute-start(f32[16,128,128]{2,1,0:T(8,128)S(1)} %get-tuple-element.24), channel_id=1, source_target_pairs={{0,48},{16,0},{32,16},{48,32},{64,112},{80,64},{96,80},{112,96},{1... | collective-permute-start | bytes 3145736 | tf_op jit(solution)/shard_map/ppermute | solution.py:259
  94.3 30.1 %collective-permute-start.15 = (f32[16,128,128]{2,1,0:T(8,128)S(1)}, f32[16,128,128]{2,1,0:T(8,128)S(1)}, u32[]{:S(2)}, u32[]{:S(2)}) collective-permute-start(f32[16,128,128]{2,1,0:T(8,128)S(1)} %get-tuple-element.30), channel_id=1, source_target_pairs={{0,64},{16,80},{32,96},{48,112},{64,0},{80,16},{96,32},{112,48},{1... | collective-permute-start | bytes 3145736 | tf_op jit(solution)/shard_map/ppermute | solution.py:263
  106.5 1.9 %collective-permute-start.11 = (f32[2,512,128]{2,1,0:T(8,128)S(1)}, f32[2,512,128]{2,1,0:T(8,128)S(1)}, u32[]{:S(2)}, u32[]{:S(2)}) collective-permute-start(f32[2,512,128]{2,1,0:T(8,128)S(1)} %collective-permute-done.9.refs_1_), channel_id=1, source_target_pairs={{0,1},{1,0},{2,3},{3,2},{4,5},{5,4},{6,7},{7,6},{8,9},{9,8},{10,11... | collective-permute-start | bytes 1572872 | tf_op jit(solution)/shard_map/ppermute | solution.py:272
  120.3 11.6 %collective-permute-start.14 = (f32[6,128,128]{2,1,0:T(8,128)S(1)}, f32[6,128,128]{2,1,0:T(8,128)S(1)}, u32[]{:S(2)}, u32[]{:S(2)}) collective-permute-start(f32[6,128,128]{2,1,0:T(8,128)S(1)} %get-tuple-element.29), channel_id=1, source_target_pairs={{0,64},{16,80},{32,96},{48,112},{64,0},{80,16},{96,32},{112,48},{1... | collective-permute-start | bytes 1179656 | tf_op jit(solution)/shard_map/ppermute | solution.py:263
  121.2 10.7 %collective-permute-start.12 = (f32[5,128,128]{2,1,0:T(8,128)S(1)}, f32[5,128,128]{2,1,0:T(8,128)S(1)}, u32[]{:S(2)}, u32[]{:S(2)}) collective-permute-start(f32[5,128,128]{2,1,0:T(8,128)S(1)} %get-tuple-element.27), channel_id=1, source_target_pairs={{0,16},{16,32},{32,48},{48,0},{64,80},{80,96},{96,112},{112,64},{1... | collective-permute-start | bytes 983048 | tf_op jit(solution)/shard_map/ppermute | solution.py:259
  121.2 10.7 %collective-permute-start.13 = (f32[5,128,128]{2,1,0:T(8,128)S(1)}, f32[5,128,128]{2,1,0:T(8,128)S(1)}, u32[]{:S(2)}, u32[]{:S(2)}) collective-permute-start(f32[5,128,128]{2,1,0:T(8,128)S(1)} %get-tuple-element.28), channel_id=1, source_target_pairs={{0,48},{16,0},{32,16},{48,32},{64,112},{80,64},{96,80},{112,96},{1... | collective-permute-start | bytes 983048 | tf_op jit(solution)/shard_map/ppermute | solution.py:259

commit v4 on v3

--- a/solution.py
+++ b/solution.py
@@ -232,7 +232,7 @@
                     )
                     out_ref[rows, columns] += both[:, :TILE] + both[:, TILE:]
 
-            pl.loop(0, count, unroll=min(count, 4))(step)
+            pl.loop(0, count, unroll=4 if count % 4 == 0 else count)(step)
             at += count
 
 

time: 137 us -> 137 us (level)
  transfers between devices with their start and end apart: 17 -> 17, of which waited for: 9 -> 9; matrix products, arithmetic and copies ran while one was open for 0% -> 0% of each run, Pallas kernels for 13% -> 14%
where the time goes in v4:
time: 137 us; the launch traced here: 136 us
  waiting for transfers between devices  73.6 us (54%)
  Pallas kernels  31.1 us (23%)
  starting transfers between devices  28.2 us (21%)
  local copies, waits for them, and re-layouts  3.16 us (2%)
    ppermute x3, waiting for transfers between devices, flip(): return lax.ppermute(value, 'col', [(c, c ^ bit) for c in range(N_COL)])  36.2 us
    ppermute x4, waiting for transfers between devices, along_x(): return lax.ppermute(value, 'col', pairs)  29.2 us
    pallas_call x3, Pallas kernels, product(): pl.pallas_call(functools.partial(product_kernel, places, start is not Non...  19.3 us
    ppermute x6, starting transfers between devices, along_z(): return lax.ppermute(value, 'row', pairs)  10.6 us
    all_to_all x1, starting transfers between devices, shards(): lax.all_to_all(sent, 'col', split_axis=0, concat_axis=0, tiled=True)  7.62 us
    ppermute x6, waiting for transfers between devices, along_z(): return lax.ppermute(value, 'row', pairs)  6.79 us
    pallas_call x1, Pallas kernels, route(): pl.pallas_call(route_kernel, out_shape=(jax.ShapeDtypeStruct((8 * STEPS,...  5.3 us
    ppermute x4, starting transfers between devices, along_x(): return lax.ppermute(value, 'col', pairs)  3.94 us
  transfers between devices with their start and end apart: 17, of which 9 were waited for; matrix products, arithmetic and copies ran while one was open for 0% of the time, Pallas kernels for 14%

profile of v4, /device:TPU:6, one launch (start us, length us, event | category | flops | bytes accessed | tf_op | source)
XLA Modules:
  0.0 136.2 jit_solution(273925448252173257)
XLA Ops:
  0.0 1.3 copy_bitcast_fusion
  1.3 5.3 %route.1 = (s32[16,128]{1,0:T(8,128)}, f32[16,2,128,128]{3,2,1,0:T(8,128)}) custom-call(s32[2,8,128]{2,1,0:T(8,128)} %bitcast.7, s32[2,8,128]{2,1,0:T(8,128)} %get-tuple-element.32.row_ref, s32[2,8,128]{2,1,0:T(8,128)} %get-tuple-element.31.column_ref, f32[2,64,128,128]{3,2,1,0:T(8,128)} %tiles_ref.1), custom_call_target="tpu_custom_call" | custom-call | tf_op jit(solution)/shard_map/route/pallas_call | solution.py:83
  6.6 7.6 %all-to-all-start = ((f32[16,2,128,128]{3,2,1,0:T(8,128)}), f32[16,2,128,128]{3,2,1,0:T(8,128)S(1)}, u32[]{:S(2)}, u32[]{:S(2)}) async-start(f32[16,2,128,128]{3,2,1,0:T(8,128)} %get-tuple-element.19), calls=%async_computation | async-start | bytes 4194304 | tf_op jit(solution)/shard_map/all_to_all | solution.py:281
  14.3 3.0 %collective-permute-start = (f32[2,512,128]{2,1,0:T(8,128)S(1)}, f32[2,512,128]{2,1,0:T(8,128)S(1)}, u32[]{:S(2)}, u32[]{:S(2)}) collective-permute-start(f32[2,512,128]{2,1,0:T(8,128)S(1)} %copy-done), channel_id=1, source_target_pairs={{0,2},{1,3},{2,0},{3,1},{4,6},{5,7},{6,4},{7,5},{8,10},{9,11},{10,... | collective-permute-start | bytes 1572872 | tf_op jit(solution)/shard_map/ppermute | solution.py:272
  17.3 0.6 collective-permute-start.1
  17.9 34.3 %collective-permute-done.side_ref = f32[2,512,128]{2,1,0:T(8,128)S(1)} collective-permute-done((f32[2,512,128]{2,1,0:T(8,128)S(1)}, f32[2,512,128]{2,1,0:T(8,128)S(1)}, u32[]{:S(2)}, u32[]{:S(2)}) %collective-permute-start) | collective-permute-done | bytes 524320 | tf_op jit(solution)/shard_map/ppermute | solution.py:272
  52.1 0.4 collective-permute-done.1.left_ref
  52.5 0.8 copy-done.1
  53.3 1.0 copy-done.2
  54.4 2.5 %compact.1 = (f32[16,128,128]{2,1,0:T(8,128)S(1)}, f32[4,512,128]{2,1,0:T(8,128)S(1)}, f32[4,512,128]{2,1,0:T(8,128)S(1)}) custom-call(s32[16,128]{1,0:T(8,128)S(1)} %copy-done.3, f32[16,2,128,128]{3,2,1,0:T(8,128)S(1)} %all-to-all-done.arrived_ref, f32[2,512,128]{2,1,0:T(8,128)S(1)} %copy-done, f32[2,512,128]{2,1,0:T(8,128)S(1)} %collective-permute-done.side_ref, ...), custom_call_target="tpu_custom_call" | custom-call | tf_op jit(solution)/shard_map/compact/pallas_call | solution.py:124
  56.9 0.5 collective-permute-start.5
  57.4 2.8 %collective-permute-start.6 = (f32[4,512,128]{2,1,0:T(8,128)S(1)}, f32[4,512,128]{2,1,0:T(8,128)S(1)}, u32[]{:S(2)}, u32[]{:S(2)}) collective-permute-start(f32[4,512,128]{2,1,0:T(8,128)S(1)} %get-tuple-element.22.refs_6_), channel_id=1, source_target_pairs={{0,4},{1,5},{2,6},{3,7},{4,8},{5,9},{6,10},{7,11},{8,12},{9,13},{1... | collective-permute-start | bytes 3145736 | tf_op jit(solution)/shard_map/ppermute | solution.py:268
  60.2 1.2 collective-permute-start.4
  61.4 4.0 %collective-permute-start.3 = (f32[16,128,128]{2,1,0:T(8,128)S(1)}, f32[16,128,128]{2,1,0:T(8,128)S(1)}, u32[]{:S(2)}, u32[]{:S(2)}) collective-permute-start(f32[16,128,128]{2,1,0:T(8,128)S(1)} %get-tuple-element.20.rest_0_), channel_id=1, source_target_pairs={{0,48},{16,0},{32,16},{48,32},{64,112},{80,64},{96,80},{112,96},{1... | collective-permute-start | bytes 3145736 | tf_op jit(solution)/shard_map/ppermute | solution.py:259
  65.4 17.4 %collective-permute-done.5.refs_4_ = f32[4,512,128]{2,1,0:T(8,128)S(1)} collective-permute-done((f32[4,512,128]{2,1,0:T(8,128)S(1)}, f32[4,512,128]{2,1,0:T(8,128)S(1)}, u32[]{:S(2)}, u32[]{:S(2)}) %collective-permute-start.5) | collective-permute-done | bytes 1048608 | tf_op jit(solution)/shard_map/ppermute | solution.py:268
  82.9 1.5 %collective-permute-done.4.refs_2_.rest_3_ = f32[16,128,128]{2,1,0:T(8,128)S(1)} collective-permute-done((f32[16,128,128]{2,1,0:T(8,128)S(1)}, f32[16,128,128]{2,1,0:T(8,128)S(1)}, u32[]{:S(2)}, u32[]{:S(2)}) %collective-permute-start.4) | collective-permute-done | bytes 1048608 | tf_op jit(solution)/shard_map/ppermute | solution.py:263
  84.4 2.5 %collective-permute-done.3.refs_1_.rest_2_ = f32[16,128,128]{2,1,0:T(8,128)S(1)} collective-permute-done((f32[16,128,128]{2,1,0:T(8,128)S(1)}, f32[16,128,128]{2,1,0:T(8,128)S(1)}, u32[]{:S(2)}, u32[]{:S(2)}) %collective-permute-start.3) | collective-permute-done | bytes 1048608 | tf_op jit(solution)/shard_map/ppermute | solution.py:259
  86.8 3.4 %collective-permute-done.2.refs_0_.rest_1_ = f32[16,128,128]{2,1,0:T(8,128)S(1)} collective-permute-done((f32[16,128,128]{2,1,0:T(8,128)S(1)}, f32[16,128,128]{2,1,0:T(8,128)S(1)}, u32[]{:S(2)}, u32[]{:S(2)}) %collective-permute-start.2) | collective-permute-done | bytes 1048608 | tf_op jit(solution)/shard_map/ppermute | solution.py:259
  90.3 0.6 regroup.2
  90.9 0.1 collective-permute-start.10
  91.1 3.2 %collective-permute-start.8 = (f32[16,128,128]{2,1,0:T(8,128)S(1)}, f32[16,128,128]{2,1,0:T(8,128)S(1)}, u32[]{:S(2)}, u32[]{:S(2)}) collective-permute-start(f32[16,128,128]{2,1,0:T(8,128)S(1)} %get-tuple-element.24), channel_id=1, source_target_pairs={{0,48},{16,0},{32,16},{48,32},{64,112},{80,64},{96,80},{112,96},{1... | collective-permute-start | bytes 3145736 | tf_op jit(solution)/shard_map/ppermute | solution.py:259
  94.4 0.8 collective-permute-start.15
  95.2 11.4 %collective-permute-done.9.refs_1_ = f32[2,512,128]{2,1,0:T(8,128)S(1)} collective-permute-done((f32[2,512,128]{2,1,0:T(8,128)S(1)}, f32[2,512,128]{2,1,0:T(8,128)S(1)}, u32[]{:S(2)}, u32[]{:S(2)}) %collective-permute-start.9) | collective-permute-done | bytes 524320 | tf_op jit(solution)/shard_map/ppermute | solution.py:268
  106.5 1.9 %collective-permute-done.11.refs_3_ = f32[2,512,128]{2,1,0:T(8,128)S(1)} collective-permute-done((f32[2,512,128]{2,1,0:T(8,128)S(1)}, f32[2,512,128]{2,1,0:T(8,128)S(1)}, u32[]{:S(2)}, u32[]{:S(2)}) %collective-permute-start.11) | collective-permute-done | bytes 524320 | tf_op jit(solution)/shard_map/ppermute | solution.py:272
  108.4 2.7 %split_amplitudes.1.rest_4_.rest_3_ = bf16[2,16,512,256]{3,2,1,0:T(8,128)(2,1)S(1)} custom-call(f32[14,512,128]{2,1,0:T(8,128)S(1)} %get-tuple-element.25.refs_0_, f32[2,512,128]{2,1,0:T(8,128)S(1)} %collective-permute-done.9.refs_1_, f32[14,512,128]{2,1,0:T(8,128)S(1)} %collective-permute-done.10.refs_2_, f32[2,512,128]{2,1,0:T(8,128)S(1)} %collective-permute-done.11.refs_3_), custom_call_target="tpu_custom_call" | custom-call | flops 1048576 | bytes 1048576 | tf_op jit(solution)/shard_map/split_amplitudes/pallas_call | solution.py:185
  111.1 8.4 %product.3.refs_2_.rest_4_ = f32[512,2048]{1,0:T(8,128)S(1)} custom-call(s32[16,128]{1,0:T(8,128)S(1)} %copy-done.3, f32[16,128,128]{2,1,0:T(8,128)S(1)} %get-tuple-element.20.rest_0_, f32[16,128,128]{2,1,0:T(8,128)S(1)} %collective-permute-done.2.refs_0_.rest_1_, f32[16,128,128]{2,1,0:T(8,128)S(1)} %collective-permute-done.3.refs_1_.rest_2_, ...), custom_call_target="tpu_custom_call" | custom-call | flops 4194304 | bytes 1048576 | tf_op jit(solution)/shard_map/product/pallas_call | solution.py:244
  119.6 0.8 regroup.3
  120.4 0.9 collective-permute-start.14
  121.2 3.2 %collective-permute-start.13 = (f32[5,128,128]{2,1,0:T(8,128)S(1)}, f32[5,128,128]{2,1,0:T(8,128)S(1)}, u32[]{:S(2)}, u32[]{:S(2)}) collective-permute-start(f32[5,128,128]{2,1,0:T(8,128)S(1)} %get-tuple-element.28), channel_id=1, source_target_pairs={{0,48},{16,0},{32,16},{48,32},{64,112},{80,64},{96,80},{112,96},{1... | collective-permute-start | bytes 983048 | tf_op jit(solution)/shard_map/ppermute | solution.py:259
  124.5 6.6 %product.4.rest_4_ = f32[512,2048]{1,0:T(8,128)S(1)} custom-call(s32[16,128]{1,0:T(8,128)S(1)} %copy-done.3, f32[16,128,128]{2,1,0:T(8,128)S(1)} %collective-permute-done.7.refs_0_.rest_0_, f32[16,128,128]{2,1,0:T(8,128)S(1)} %collective-permute-done.8.refs_1_.rest_1_, f32[16,128,128]{2,1,0:T(8,128)S(1)} %collective-permute-done.15.rest_2_, ...), custom_call_target="tpu_custom_call" | custom-call | flops 3145728 | bytes 1048576 | tf_op jit(solution)/shard_map/product/pallas_call | solution.py:244
  131.1 0.9 collective-permute-done.12.rest_0_
  131.9 4.3 %product.5 = f32[512,2048]{1,0:T(8,128)} custom-call(s32[16,128]{1,0:T(8,128)S(1)} %copy-done.3, f32[5,128,128]{2,1,0:T(8,128)S(1)} %collective-permute-done.12.rest_0_, f32[5,128,128]{2,1,0:T(8,128)S(1)} %collective-permute-done.13.rest_1_, f32[6,128,128]{2,1,0:T(8,128)S(1)} %collective-permute-done.14.rest_2_, ...), custom_call_target="tpu_custom_call" | custom-call | flops 1048576 | bytes 1048576 | tf_op jit(solution)/shard_map/product/pallas_call | solution.py:244
  (19 shorter events, 0.2 us)
Async XLA Ops:
  6.6 7.6 %copy-start = (f32[2,512,128]{2,1,0:T(8,128)S(1)}, f32[2,512,128]{2,1,0:T(8,128)}, u32[]{:S(2)}) copy-start(f32[2,512,128]{2,1,0:T(8,128)} %amp_ref.1) | copy-start | bytes 1572868
  6.6 46.7 %copy-start.3 = (s32[16,128]{1,0:T(8,128)S(1)}, s32[16,128]{1,0:T(8,128)}, u32[]{:S(2)}) copy-start(s32[16,128]{1,0:T(8,128)} %get-tuple-element.18.meta_ref) | copy-start | bytes 24580
  6.6 46.7 %all-to-all-start = ((f32[16,2,128,128]{3,2,1,0:T(8,128)}), f32[16,2,128,128]{3,2,1,0:T(8,128)S(1)}, u32[]{:S(2)}, u32[]{:S(2)}) async-start(f32[16,2,128,128]{3,2,1,0:T(8,128)} %get-tuple-element.19), calls=%async_computation | async-start | bytes 4194304 | tf_op jit(solution)/shard_map/all_to_all | solution.py:281
  14.3 37.9 %collective-permute-start = (f32[2,512,128]{2,1,0:T(8,128)S(1)}, f32[2,512,128]{2,1,0:T(8,128)S(1)}, u32[]{:S(2)}, u32[]{:S(2)}) collective-permute-start(f32[2,512,128]{2,1,0:T(8,128)S(1)} %copy-done), channel_id=1, source_target_pairs={{0,2},{1,3},{2,0},{3,1},{4,6},{5,7},{6,4},{7,5},{8,10},{9,11},{10,... | collective-permute-start | bytes 1572872 | tf_op jit(solution)/shard_map/ppermute | solution.py:272
  17.3 35.2 %collective-permute-start.1 = (f32[2,512,128]{2,1,0:T(8,128)S(1)}, f32[2,512,128]{2,1,0:T(8,128)S(1)}, u32[]{:S(2)}, u32[]{:S(2)}) collective-permute-start(f32[2,512,128]{2,1,0:T(8,128)S(1)} %copy-done), channel_id=1, source_target_pairs={{0,4},{1,5},{2,6},{3,7},{4,8},{5,9},{6,10},{7,11},{8,12},{9,13},{1... | collective-permute-start | bytes 1572872 | tf_op jit(solution)/shard_map/ppermute | solution.py:268
  52.5 0.8 copy-start.1
  53.3 1.0 copy-start.2
  56.9 26.0 %collective-permute-start.5 = (f32[4,512,128]{2,1,0:T(8,128)S(1)}, f32[4,512,128]{2,1,0:T(8,128)S(1)}, u32[]{:S(2)}, u32[]{:S(2)}) collective-permute-start(f32[4,512,128]{2,1,0:T(8,128)S(1)} %get-tuple-element.21.refs_3_), channel_id=1, source_target_pairs={{0,12},{1,13},{2,14},{3,15},{4,0},{5,1},{6,2},{7,3},{8,4},{9,5},{1... | collective-permute-start | bytes 3145736 | tf_op jit(solution)/shard_map/ppermute | solution.py:268
  57.4 25.5 %collective-permute-start.6 = (f32[4,512,128]{2,1,0:T(8,128)S(1)}, f32[4,512,128]{2,1,0:T(8,128)S(1)}, u32[]{:S(2)}, u32[]{:S(2)}) collective-permute-start(f32[4,512,128]{2,1,0:T(8,128)S(1)} %get-tuple-element.22.refs_6_), channel_id=1, source_target_pairs={{0,4},{1,5},{2,6},{3,7},{4,8},{5,9},{6,10},{7,11},{8,12},{9,13},{1... | collective-permute-start | bytes 3145736 | tf_op jit(solution)/shard_map/ppermute | solution.py:268
  60.2 24.2 %collective-permute-start.4 = (f32[16,128,128]{2,1,0:T(8,128)S(1)}, f32[16,128,128]{2,1,0:T(8,128)S(1)}, u32[]{:S(2)}, u32[]{:S(2)}) collective-permute-start(f32[16,128,128]{2,1,0:T(8,128)S(1)} %get-tuple-element.20.rest_0_), channel_id=1, source_target_pairs={{0,64},{16,80},{32,96},{48,112},{64,0},{80,16},{96,32},{112,48},{1... | collective-permute-start | bytes 3145736 | tf_op jit(solution)/shard_map/ppermute | solution.py:263
  61.4 25.5 %collective-permute-start.3 = (f32[16,128,128]{2,1,0:T(8,128)S(1)}, f32[16,128,128]{2,1,0:T(8,128)S(1)}, u32[]{:S(2)}, u32[]{:S(2)}) collective-permute-start(f32[16,128,128]{2,1,0:T(8,128)S(1)} %get-tuple-element.20.rest_0_), channel_id=1, source_target_pairs={{0,48},{16,0},{32,16},{48,32},{64,112},{80,64},{96,80},{112,96},{1... | collective-permute-start | bytes 3145736 | tf_op jit(solution)/shard_map/ppermute | solution.py:259
  65.4 24.8 %collective-permute-start.2 = (f32[16,128,128]{2,1,0:T(8,128)S(1)}, f32[16,128,128]{2,1,0:T(8,128)S(1)}, u32[]{:S(2)}, u32[]{:S(2)}) collective-permute-start(f32[16,128,128]{2,1,0:T(8,128)S(1)} %get-tuple-element.20.rest_0_), channel_id=1, source_target_pairs={{0,16},{16,32},{32,48},{48,0},{64,80},{80,96},{96,112},{112,64},{1... | collective-permute-start | bytes 3145736 | tf_op jit(solution)/shard_map/ppermute | solution.py:259
  90.9 17.6 %collective-permute-start.10 = (f32[14,512,128]{2,1,0:T(8,128)S(1)}, f32[14,512,128]{2,1,0:T(8,128)S(1)}, u32[]{:S(2)}, u32[]{:S(2)}) collective-permute-start(f32[14,512,128]{2,1,0:T(8,128)S(1)} %get-tuple-element.25.refs_0_), channel_id=1, source_target_pairs={{0,1},{1,0},{2,3},{3,2},{4,5},{5,4},{6,7},{7,6},{8,9},{9,8},{10,11... | collective-permute-start | bytes 11010056 | tf_op jit(solution)/shard_map/ppermute | solution.py:272
  91.0 15.6 %collective-permute-start.9 = (f32[2,512,128]{2,1,0:T(8,128)S(1)}, f32[2,512,128]{2,1,0:T(8,128)S(1)}, u32[]{:S(2)}, u32[]{:S(2)}) collective-permute-start(f32[2,512,128]{2,1,0:T(8,128)S(1)} %get-tuple-element.26), channel_id=1, source_target_pairs={{0,12},{1,13},{2,14},{3,15},{4,0},{5,1},{6,2},{7,3},{8,4},{9,5},{1... | collective-permute-start | bytes 1572872 | tf_op jit(solution)/shard_map/ppermute | solution.py:268
  91.1 28.5 %collective-permute-start.7 = (f32[16,128,128]{2,1,0:T(8,128)S(1)}, f32[16,128,128]{2,1,0:T(8,128)S(1)}, u32[]{:S(2)}, u32[]{:S(2)}) collective-permute-start(f32[16,128,128]{2,1,0:T(8,128)S(1)} %get-tuple-element.23), channel_id=1, source_target_pairs={{0,16},{16,32},{32,48},{48,0},{64,80},{80,96},{96,112},{112,64},{1... | collective-permute-start | bytes 3145736 | tf_op jit(solution)/shard_map/ppermute | solution.py:259
  91.1 28.4 %collective-permute-start.8 = (f32[16,128,128]{2,1,0:T(8,128)S(1)}, f32[16,128,128]{2,1,0:T(8,128)S(1)}, u32[]{:S(2)}, u32[]{:S(2)}) collective-permute-start(f32[16,128,128]{2,1,0:T(8,128)S(1)} %get-tuple-element.24), channel_id=1, source_target_pairs={{0,48},{16,0},{32,16},{48,32},{64,112},{80,64},{96,80},{112,96},{1... | collective-permute-start | bytes 3145736 | tf_op jit(solution)/shard_map/ppermute | solution.py:259
  94.4 30.1 %collective-permute-start.15 = (f32[16,128,128]{2,1,0:T(8,128)S(1)}, f32[16,128,128]{2,1,0:T(8,128)S(1)}, u32[]{:S(2)}, u32[]{:S(2)}) collective-permute-start(f32[16,128,128]{2,1,0:T(8,128)S(1)} %get-tuple-element.30), channel_id=1, source_target_pairs={{0,64},{16,80},{32,96},{48,112},{64,0},{80,16},{96,32},{112,48},{1... | collective-permute-start | bytes 3145736 | tf_op jit(solution)/shard_map/ppermute | solution.py:263
  106.5 1.9 %collective-permute-start.11 = (f32[2,512,128]{2,1,0:T(8,128)S(1)}, f32[2,512,128]{2,1,0:T(8,128)S(1)}, u32[]{:S(2)}, u32[]{:S(2)}) collective-permute-start(f32[2,512,128]{2,1,0:T(8,128)S(1)} %collective-permute-done.9.refs_1_), channel_id=1, source_target_pairs={{0,1},{1,0},{2,3},{3,2},{4,5},{5,4},{6,7},{7,6},{8,9},{9,8},{10,11... | collective-permute-start | bytes 1572872 | tf_op jit(solution)/shard_map/ppermute | solution.py:272
  120.4 11.6 %collective-permute-start.14 = (f32[6,128,128]{2,1,0:T(8,128)S(1)}, f32[6,128,128]{2,1,0:T(8,128)S(1)}, u32[]{:S(2)}, u32[]{:S(2)}) collective-permute-start(f32[6,128,128]{2,1,0:T(8,128)S(1)} %get-tuple-element.29), channel_id=1, source_target_pairs={{0,64},{16,80},{32,96},{48,112},{64,0},{80,16},{96,32},{112,48},{1... | collective-permute-start | bytes 1179656 | tf_op jit(solution)/shard_map/ppermute | solution.py:263
  121.2 10.7 %collective-permute-start.12 = (f32[5,128,128]{2,1,0:T(8,128)S(1)}, f32[5,128,128]{2,1,0:T(8,128)S(1)}, u32[]{:S(2)}, u32[]{:S(2)}) collective-permute-start(f32[5,128,128]{2,1,0:T(8,128)S(1)} %get-tuple-element.27), channel_id=1, source_target_pairs={{0,16},{16,32},{32,48},{48,0},{64,80},{80,96},{96,112},{112,64},{1... | collective-permute-start | bytes 983048 | tf_op jit(solution)/shard_map/ppermute | solution.py:259
  121.2 10.7 %collective-permute-start.13 = (f32[5,128,128]{2,1,0:T(8,128)S(1)}, f32[5,128,128]{2,1,0:T(8,128)S(1)}, u32[]{:S(2)}, u32[]{:S(2)}) collective-permute-start(f32[5,128,128]{2,1,0:T(8,128)S(1)} %get-tuple-element.28), channel_id=1, source_target_pairs={{0,48},{16,0},{32,16},{48,32},{64,112},{80,64},{96,80},{112,96},{1... | collective-permute-start | bytes 983048 | tf_op jit(solution)/shard_map/ppermute | solution.py:259

commit v5 on v4

--- a/solution.py
+++ b/solution.py
@@ -57,7 +57,8 @@
             send = send + jnp.where(sent, (held % HOLD).astype(jnp.float32), 0.0)
             place = jnp.sum(jnp.where(named[g], number, 0), axis=0, keepdims=True)
             mine = (place == numbers) & (readers[g : g + 1] == me_col)
-            tile_code = row_ref[s, g : g + 1] * NT_DEV + column_ref[s, g : g + 1]
+            panel, lanes = slice(s, s + 1), slice(g * LANES, (g + 1) * LANES)
+            tile_code = row_ref[panel, lanes] * NT_DEV + column_ref[panel, lanes]
             code = code + jnp.where(mine, tile_code.astype(jnp.float32), 0.0)
             holder = holder + jnp.where(mine, (held // HOLD).astype(jnp.float32), 0.0)
         parts = [to_lanes(code)[:1], to_lanes(holder)[:1], to_lanes(send)[:1]]
@@ -275,7 +276,7 @@
 def shards(amplitudes, integrals, tile_rows, tile_reader, tile_column):
     held = (STEPS, tile_rows.shape[1] // LANES, LANES)
     meta, sent = route(
-        tile_reader.reshape(held), tile_rows.reshape(held), tile_column.reshape(held), integrals
+        tile_reader.reshape(held), tile_rows, tile_column, integrals
     )
     side, amp_left = flip(amplitudes, 2), along_x(amplitudes, 1)
     arrived = lax.all_to_all(sent, "col", split_axis=0, concat_axis=0, tiled=True)

time: 137 us -> 135 us (0.985)
  no operation moved by 1% of the time
where the time goes in v5:
time: 135 us
  waiting for transfers between devices  73.5 us (54%)
  Pallas kernels  31.2 us (23%)
  starting transfers between devices  28.4 us (21%)
  local copies, waits for them, and re-layouts  1.86 us (1%)
    ppermute x3, waiting for transfers between devices, flip(): return lax.ppermute(value, 'col', [(c, c ^ bit) for c in range(N_COL)])  36.2 us
    ppermute x4, waiting for transfers between devices, along_x(): return lax.ppermute(value, 'col', pairs)  29.1 us
    pallas_call x3, Pallas kernels, product(): pl.pallas_call(functools.partial(product_kernel, places, start is not Non...  19.4 us
    ppermute x6, starting transfers between devices, along_z(): return lax.ppermute(value, 'row', pairs)  10.5 us
    all_to_all x1, starting transfers between devices, shards(): lax.all_to_all(sent, 'col', split_axis=0, concat_axis=0, tiled=True)  7.61 us
    ppermute x6, waiting for transfers between devices, along_z(): return lax.ppermute(value, 'row', pairs)  6.71 us
    pallas_call x1, Pallas kernels, route(): pl.pallas_call(route_kernel, out_shape=(jax.ShapeDtypeStruct((8 * STEPS,...  5.3 us
    ppermute x4, starting transfers between devices, along_x(): return lax.ppermute(value, 'col', pairs)  3.94 us
  transfers between devices with their start and end apart: 17, of which 9 were waited for; matrix products, arithmetic and copies ran while one was open for 0% of the time, Pallas kernels for 14%

profile of v5, /device:TPU:6, one launch (start us, length us, event | category | flops | bytes accessed | tf_op | source)
XLA Modules:
  0.0 135.0 jit_solution(10773443470497415980)
XLA Ops:
  0.0 5.3 %route.1 = (s32[16,128]{1,0:T(8,128)}, f32[16,2,128,128]{3,2,1,0:T(8,128)}) custom-call(s32[2,8,128]{2,1,0:T(8,128)} %bitcast.1, s32[2,1024]{1,0:T(2,128)} %row_ref.1, s32[2,1024]{1,0:T(2,128)} %column_ref.1, f32[2,64,128,128]{3,2,1,0:T(8,128)} %tiles_ref.1), custom_call_target="tpu_custom_call" | custom-call | tf_op jit(solution)/shard_map/route/pallas_call | solution.py:84
  5.3 7.6 %all-to-all-start = ((f32[16,2,128,128]{3,2,1,0:T(8,128)}), f32[16,2,128,128]{3,2,1,0:T(8,128)S(1)}, u32[]{:S(2)}, u32[]{:S(2)}) async-start(f32[16,2,128,128]{3,2,1,0:T(8,128)} %get-tuple-element.19), calls=%async_computation | async-start | bytes 4194304 | tf_op jit(solution)/shard_map/all_to_all | solution.py:282
  13.0 3.0 %collective-permute-start = (f32[2,512,128]{2,1,0:T(8,128)S(1)}, f32[2,512,128]{2,1,0:T(8,128)S(1)}, u32[]{:S(2)}, u32[]{:S(2)}) collective-permute-start(f32[2,512,128]{2,1,0:T(8,128)S(1)} %copy-done), channel_id=1, source_target_pairs={{0,2},{1,3},{2,0},{3,1},{4,6},{5,7},{6,4},{7,5},{8,10},{9,11},{10,... | collective-permute-start | bytes 1572872 | tf_op jit(solution)/shard_map/ppermute | solution.py:273
  16.0 0.6 collective-permute-start.1
  16.6 34.3 %collective-permute-done.side_ref = f32[2,512,128]{2,1,0:T(8,128)S(1)} collective-permute-done((f32[2,512,128]{2,1,0:T(8,128)S(1)}, f32[2,512,128]{2,1,0:T(8,128)S(1)}, u32[]{:S(2)}, u32[]{:S(2)}) %collective-permute-start) | collective-permute-done | bytes 524320 | tf_op jit(solution)/shard_map/ppermute | solution.py:273
  50.8 0.4 collective-permute-done.1.left_ref
  51.2 0.8 copy-done.1
  52.0 1.0 copy-done.2
  53.1 2.5 %compact.1 = (f32[16,128,128]{2,1,0:T(8,128)S(1)}, f32[4,512,128]{2,1,0:T(8,128)S(1)}, f32[4,512,128]{2,1,0:T(8,128)S(1)}) custom-call(s32[16,128]{1,0:T(8,128)S(1)} %copy-done.3, f32[16,2,128,128]{3,2,1,0:T(8,128)S(1)} %all-to-all-done.arrived_ref, f32[2,512,128]{2,1,0:T(8,128)S(1)} %copy-done, f32[2,512,128]{2,1,0:T(8,128)S(1)} %collective-permute-done.side_ref, ...), custom_call_target="tpu_custom_call" | custom-call | tf_op jit(solution)/shard_map/compact/pallas_call | solution.py:125
  55.6 0.5 collective-permute-start.5
  56.1 2.8 %collective-permute-start.6 = (f32[4,512,128]{2,1,0:T(8,128)S(1)}, f32[4,512,128]{2,1,0:T(8,128)S(1)}, u32[]{:S(2)}, u32[]{:S(2)}) collective-permute-start(f32[4,512,128]{2,1,0:T(8,128)S(1)} %get-tuple-element.22.refs_6_), channel_id=1, source_target_pairs={{0,4},{1,5},{2,6},{3,7},{4,8},{5,9},{6,10},{7,11},{8,12},{9,13},{1... | collective-permute-start | bytes 3145736 | tf_op jit(solution)/shard_map/ppermute | solution.py:269
  58.9 1.2 collective-permute-start.4
  60.0 4.0 %collective-permute-start.3 = (f32[16,128,128]{2,1,0:T(8,128)S(1)}, f32[16,128,128]{2,1,0:T(8,128)S(1)}, u32[]{:S(2)}, u32[]{:S(2)}) collective-permute-start(f32[16,128,128]{2,1,0:T(8,128)S(1)} %get-tuple-element.20.rest_0_), channel_id=1, source_target_pairs={{0,48},{16,0},{32,16},{48,32},{64,112},{80,64},{96,80},{112,96},{1... | collective-permute-start | bytes 3145736 | tf_op jit(solution)/shard_map/ppermute | solution.py:260
  64.1 17.5 %collective-permute-done.5.refs_4_ = f32[4,512,128]{2,1,0:T(8,128)S(1)} collective-permute-done((f32[4,512,128]{2,1,0:T(8,128)S(1)}, f32[4,512,128]{2,1,0:T(8,128)S(1)}, u32[]{:S(2)}, u32[]{:S(2)}) %collective-permute-start.5) | collective-permute-done | bytes 1048608 | tf_op jit(solution)/shard_map/ppermute | solution.py:269
  81.6 1.5 %collective-permute-done.4.refs_2_.rest_3_ = f32[16,128,128]{2,1,0:T(8,128)S(1)} collective-permute-done((f32[16,128,128]{2,1,0:T(8,128)S(1)}, f32[16,128,128]{2,1,0:T(8,128)S(1)}, u32[]{:S(2)}, u32[]{:S(2)}) %collective-permute-start.4) | collective-permute-done | bytes 1048608 | tf_op jit(solution)/shard_map/ppermute | solution.py:264
  83.0 2.4 %collective-permute-done.3.refs_1_.rest_2_ = f32[16,128,128]{2,1,0:T(8,128)S(1)} collective-permute-done((f32[16,128,128]{2,1,0:T(8,128)S(1)}, f32[16,128,128]{2,1,0:T(8,128)S(1)}, u32[]{:S(2)}, u32[]{:S(2)}) %collective-permute-start.3) | collective-permute-done | bytes 1048608 | tf_op jit(solution)/shard_map/ppermute | solution.py:260
  85.5 3.4 %collective-permute-done.2.refs_0_.rest_1_ = f32[16,128,128]{2,1,0:T(8,128)S(1)} collective-permute-done((f32[16,128,128]{2,1,0:T(8,128)S(1)}, f32[16,128,128]{2,1,0:T(8,128)S(1)}, u32[]{:S(2)}, u32[]{:S(2)}) %collective-permute-start.2) | collective-permute-done | bytes 1048608 | tf_op jit(solution)/shard_map/ppermute | solution.py:260
  88.9 0.6 regroup.2
  89.5 0.1 collective-permute-start.10
  89.7 0.1 collective-permute-start.7
  89.8 3.2 %collective-permute-start.8 = (f32[16,128,128]{2,1,0:T(8,128)S(1)}, f32[16,128,128]{2,1,0:T(8,128)S(1)}, u32[]{:S(2)}, u32[]{:S(2)}) collective-permute-start(f32[16,128,128]{2,1,0:T(8,128)S(1)} %get-tuple-element.24), channel_id=1, source_target_pairs={{0,48},{16,0},{32,16},{48,32},{64,112},{80,64},{96,80},{112,96},{1... | collective-permute-start | bytes 3145736 | tf_op jit(solution)/shard_map/ppermute | solution.py:260
  93.0 1.0 collective-permute-start.15
  94.0 11.2 %collective-permute-done.9.refs_1_ = f32[2,512,128]{2,1,0:T(8,128)S(1)} collective-permute-done((f32[2,512,128]{2,1,0:T(8,128)S(1)}, f32[2,512,128]{2,1,0:T(8,128)S(1)}, u32[]{:S(2)}, u32[]{:S(2)}) %collective-permute-start.9) | collective-permute-done | bytes 524320 | tf_op jit(solution)/shard_map/ppermute | solution.py:269
  105.2 1.9 %collective-permute-done.11.refs_3_ = f32[2,512,128]{2,1,0:T(8,128)S(1)} collective-permute-done((f32[2,512,128]{2,1,0:T(8,128)S(1)}, f32[2,512,128]{2,1,0:T(8,128)S(1)}, u32[]{:S(2)}, u32[]{:S(2)}) %collective-permute-start.11) | collective-permute-done | bytes 524320 | tf_op jit(solution)/shard_map/ppermute | solution.py:273
  107.1 2.7 %split_amplitudes.1.rest_4_.rest_3_ = bf16[2,16,512,256]{3,2,1,0:T(8,128)(2,1)S(1)} custom-call(f32[14,512,128]{2,1,0:T(8,128)S(1)} %get-tuple-element.25.refs_0_, f32[2,512,128]{2,1,0:T(8,128)S(1)} %collective-permute-done.9.refs_1_, f32[14,512,128]{2,1,0:T(8,128)S(1)} %collective-permute-done.10.refs_2_, f32[2,512,128]{2,1,0:T(8,128)S(1)} %collective-permute-done.11.refs_3_), custom_call_target="tpu_custom_call" | custom-call | flops 1048576 | bytes 1048576 | tf_op jit(solution)/shard_map/split_amplitudes/pallas_call | solution.py:186
  109.7 8.5 %product.3.refs_2_.rest_4_ = f32[512,2048]{1,0:T(8,128)S(1)} custom-call(s32[16,128]{1,0:T(8,128)S(1)} %copy-done.3, f32[16,128,128]{2,1,0:T(8,128)S(1)} %get-tuple-element.20.rest_0_, f32[16,128,128]{2,1,0:T(8,128)S(1)} %collective-permute-done.2.refs_0_.rest_1_, f32[16,128,128]{2,1,0:T(8,128)S(1)} %collective-permute-done.3.refs_1_.rest_2_, ...), custom_call_target="tpu_custom_call" | custom-call | flops 4194304 | bytes 1048576 | tf_op jit(solution)/shard_map/product/pallas_call | solution.py:245
  118.2 0.8 regroup.3
  119.0 1.0 collective-permute-start.14
  120.0 3.2 %collective-permute-start.13 = (f32[5,128,128]{2,1,0:T(8,128)S(1)}, f32[5,128,128]{2,1,0:T(8,128)S(1)}, u32[]{:S(2)}, u32[]{:S(2)}) collective-permute-start(f32[5,128,128]{2,1,0:T(8,128)S(1)} %get-tuple-element.28), channel_id=1, source_target_pairs={{0,48},{16,0},{32,16},{48,32},{64,112},{80,64},{96,80},{112,96},{1... | collective-permute-start | bytes 983048 | tf_op jit(solution)/shard_map/ppermute | solution.py:260
  123.3 6.6 %product.4.rest_4_ = f32[512,2048]{1,0:T(8,128)S(1)} custom-call(s32[16,128]{1,0:T(8,128)S(1)} %copy-done.3, f32[16,128,128]{2,1,0:T(8,128)S(1)} %collective-permute-done.7.refs_0_.rest_0_, f32[16,128,128]{2,1,0:T(8,128)S(1)} %collective-permute-done.8.refs_1_.rest_1_, f32[16,128,128]{2,1,0:T(8,128)S(1)} %collective-permute-done.15.rest_2_, ...), custom_call_target="tpu_custom_call" | custom-call | flops 3145728 | bytes 1048576 | tf_op jit(solution)/shard_map/product/pallas_call | solution.py:245
  129.9 0.9 collective-permute-done.12.rest_0_
  130.7 4.3 %product.5 = f32[512,2048]{1,0:T(8,128)} custom-call(s32[16,128]{1,0:T(8,128)S(1)} %copy-done.3, f32[5,128,128]{2,1,0:T(8,128)S(1)} %collective-permute-done.12.rest_0_, f32[5,128,128]{2,1,0:T(8,128)S(1)} %collective-permute-done.13.rest_1_, f32[6,128,128]{2,1,0:T(8,128)S(1)} %collective-permute-done.14.rest_2_, ...), custom_call_target="tpu_custom_call" | custom-call | flops 1048576 | bytes 1048576 | tf_op jit(solution)/shard_map/product/pallas_call | solution.py:245
  (18 shorter events, 0.1 us)
Async XLA Ops:
  5.3 7.6 %copy-start = (f32[2,512,128]{2,1,0:T(8,128)S(1)}, f32[2,512,128]{2,1,0:T(8,128)}, u32[]{:S(2)}) copy-start(f32[2,512,128]{2,1,0:T(8,128)} %amp_ref.1) | copy-start | bytes 1572868
  5.3 46.7 %copy-start.3 = (s32[16,128]{1,0:T(8,128)S(1)}, s32[16,128]{1,0:T(8,128)}, u32[]{:S(2)}) copy-start(s32[16,128]{1,0:T(8,128)} %get-tuple-element.18.meta_ref) | copy-start | bytes 24580
  5.3 46.7 %all-to-all-start = ((f32[16,2,128,128]{3,2,1,0:T(8,128)}), f32[16,2,128,128]{3,2,1,0:T(8,128)S(1)}, u32[]{:S(2)}, u32[]{:S(2)}) async-start(f32[16,2,128,128]{3,2,1,0:T(8,128)} %get-tuple-element.19), calls=%async_computation | async-start | bytes 4194304 | tf_op jit(solution)/shard_map/all_to_all | solution.py:282
  13.0 37.9 %collective-permute-start = (f32[2,512,128]{2,1,0:T(8,128)S(1)}, f32[2,512,128]{2,1,0:T(8,128)S(1)}, u32[]{:S(2)}, u32[]{:S(2)}) collective-permute-start(f32[2,512,128]{2,1,0:T(8,128)S(1)} %copy-done), channel_id=1, source_target_pairs={{0,2},{1,3},{2,0},{3,1},{4,6},{5,7},{6,4},{7,5},{8,10},{9,11},{10,... | collective-permute-start | bytes 1572872 | tf_op jit(solution)/shard_map/ppermute | solution.py:273
  16.0 35.2 %collective-permute-start.1 = (f32[2,512,128]{2,1,0:T(8,128)S(1)}, f32[2,512,128]{2,1,0:T(8,128)S(1)}, u32[]{:S(2)}, u32[]{:S(2)}) collective-permute-start(f32[2,512,128]{2,1,0:T(8,128)S(1)} %copy-done), channel_id=1, source_target_pairs={{0,4},{1,5},{2,6},{3,7},{4,8},{5,9},{6,10},{7,11},{8,12},{9,13},{1... | collective-permute-start | bytes 1572872 | tf_op jit(solution)/shard_map/ppermute | solution.py:269
  51.2 0.8 copy-start.1
  52.0 1.0 copy-start.2
  55.6 26.0 %collective-permute-start.5 = (f32[4,512,128]{2,1,0:T(8,128)S(1)}, f32[4,512,128]{2,1,0:T(8,128)S(1)}, u32[]{:S(2)}, u32[]{:S(2)}) collective-permute-start(f32[4,512,128]{2,1,0:T(8,128)S(1)} %get-tuple-element.21.refs_3_), channel_id=1, source_target_pairs={{0,12},{1,13},{2,14},{3,15},{4,0},{5,1},{6,2},{7,3},{8,4},{9,5},{1... | collective-permute-start | bytes 3145736 | tf_op jit(solution)/shard_map/ppermute | solution.py:269
  56.1 25.5 %collective-permute-start.6 = (f32[4,512,128]{2,1,0:T(8,128)S(1)}, f32[4,512,128]{2,1,0:T(8,128)S(1)}, u32[]{:S(2)}, u32[]{:S(2)}) collective-permute-start(f32[4,512,128]{2,1,0:T(8,128)S(1)} %get-tuple-element.22.refs_6_), channel_id=1, source_target_pairs={{0,4},{1,5},{2,6},{3,7},{4,8},{5,9},{6,10},{7,11},{8,12},{9,13},{1... | collective-permute-start | bytes 3145736 | tf_op jit(solution)/shard_map/ppermute | solution.py:269
  58.9 24.2 %collective-permute-start.4 = (f32[16,128,128]{2,1,0:T(8,128)S(1)}, f32[16,128,128]{2,1,0:T(8,128)S(1)}, u32[]{:S(2)}, u32[]{:S(2)}) collective-permute-start(f32[16,128,128]{2,1,0:T(8,128)S(1)} %get-tuple-element.20.rest_0_), channel_id=1, source_target_pairs={{0,64},{16,80},{32,96},{48,112},{64,0},{80,16},{96,32},{112,48},{1... | collective-permute-start | bytes 3145736 | tf_op jit(solution)/shard_map/ppermute | solution.py:264
  60.0 25.4 %collective-permute-start.3 = (f32[16,128,128]{2,1,0:T(8,128)S(1)}, f32[16,128,128]{2,1,0:T(8,128)S(1)}, u32[]{:S(2)}, u32[]{:S(2)}) collective-permute-start(f32[16,128,128]{2,1,0:T(8,128)S(1)} %get-tuple-element.20.rest_0_), channel_id=1, source_target_pairs={{0,48},{16,0},{32,16},{48,32},{64,112},{80,64},{96,80},{112,96},{1... | collective-permute-start | bytes 3145736 | tf_op jit(solution)/shard_map/ppermute | solution.py:260
  64.1 24.8 %collective-permute-start.2 = (f32[16,128,128]{2,1,0:T(8,128)S(1)}, f32[16,128,128]{2,1,0:T(8,128)S(1)}, u32[]{:S(2)}, u32[]{:S(2)}) collective-permute-start(f32[16,128,128]{2,1,0:T(8,128)S(1)} %get-tuple-element.20.rest_0_), channel_id=1, source_target_pairs={{0,16},{16,32},{32,48},{48,0},{64,80},{80,96},{96,112},{112,64},{1... | collective-permute-start | bytes 3145736 | tf_op jit(solution)/shard_map/ppermute | solution.py:260
  89.5 17.6 %collective-permute-start.10 = (f32[14,512,128]{2,1,0:T(8,128)S(1)}, f32[14,512,128]{2,1,0:T(8,128)S(1)}, u32[]{:S(2)}, u32[]{:S(2)}) collective-permute-start(f32[14,512,128]{2,1,0:T(8,128)S(1)} %get-tuple-element.25.refs_0_), channel_id=1, source_target_pairs={{0,1},{1,0},{2,3},{3,2},{4,5},{5,4},{6,7},{7,6},{8,9},{9,8},{10,11... | collective-permute-start | bytes 11010056 | tf_op jit(solution)/shard_map/ppermute | solution.py:273
  89.6 15.6 %collective-permute-start.9 = (f32[2,512,128]{2,1,0:T(8,128)S(1)}, f32[2,512,128]{2,1,0:T(8,128)S(1)}, u32[]{:S(2)}, u32[]{:S(2)}) collective-permute-start(f32[2,512,128]{2,1,0:T(8,128)S(1)} %get-tuple-element.26), channel_id=1, source_target_pairs={{0,12},{1,13},{2,14},{3,15},{4,0},{5,1},{6,2},{7,3},{8,4},{9,5},{1... | collective-permute-start | bytes 1572872 | tf_op jit(solution)/shard_map/ppermute | solution.py:269
  89.7 28.5 %collective-permute-start.7 = (f32[16,128,128]{2,1,0:T(8,128)S(1)}, f32[16,128,128]{2,1,0:T(8,128)S(1)}, u32[]{:S(2)}, u32[]{:S(2)}) collective-permute-start(f32[16,128,128]{2,1,0:T(8,128)S(1)} %get-tuple-element.23), channel_id=1, source_target_pairs={{0,16},{16,32},{32,48},{48,0},{64,80},{80,96},{96,112},{112,64},{1... | collective-permute-start | bytes 3145736 | tf_op jit(solution)/shard_map/ppermute | solution.py:260
  89.8 28.5 %collective-permute-start.8 = (f32[16,128,128]{2,1,0:T(8,128)S(1)}, f32[16,128,128]{2,1,0:T(8,128)S(1)}, u32[]{:S(2)}, u32[]{:S(2)}) collective-permute-start(f32[16,128,128]{2,1,0:T(8,128)S(1)} %get-tuple-element.24), channel_id=1, source_target_pairs={{0,48},{16,0},{32,16},{48,32},{64,112},{80,64},{96,80},{112,96},{1... | collective-permute-start | bytes 3145736 | tf_op jit(solution)/shard_map/ppermute | solution.py:260
  93.0 30.3 %collective-permute-start.15 = (f32[16,128,128]{2,1,0:T(8,128)S(1)}, f32[16,128,128]{2,1,0:T(8,128)S(1)}, u32[]{:S(2)}, u32[]{:S(2)}) collective-permute-start(f32[16,128,128]{2,1,0:T(8,128)S(1)} %get-tuple-element.30), channel_id=1, source_target_pairs={{0,64},{16,80},{32,96},{48,112},{64,0},{80,16},{96,32},{112,48},{1... | collective-permute-start | bytes 3145736 | tf_op jit(solution)/shard_map/ppermute | solution.py:264
  105.2 1.9 %collective-permute-start.11 = (f32[2,512,128]{2,1,0:T(8,128)S(1)}, f32[2,512,128]{2,1,0:T(8,128)S(1)}, u32[]{:S(2)}, u32[]{:S(2)}) collective-permute-start(f32[2,512,128]{2,1,0:T(8,128)S(1)} %collective-permute-done.9.refs_1_), channel_id=1, source_target_pairs={{0,1},{1,0},{2,3},{3,2},{4,5},{5,4},{6,7},{7,6},{8,9},{9,8},{10,11... | collective-permute-start | bytes 1572872 | tf_op jit(solution)/shard_map/ppermute | solution.py:273
  119.0 11.7 %collective-permute-start.14 = (f32[6,128,128]{2,1,0:T(8,128)S(1)}, f32[6,128,128]{2,1,0:T(8,128)S(1)}, u32[]{:S(2)}, u32[]{:S(2)}) collective-permute-start(f32[6,128,128]{2,1,0:T(8,128)S(1)} %get-tuple-element.29), channel_id=1, source_target_pairs={{0,64},{16,80},{32,96},{48,112},{64,0},{80,16},{96,32},{112,48},{1... | collective-permute-start | bytes 1179656 | tf_op jit(solution)/shard_map/ppermute | solution.py:264
  120.0 10.7 %collective-permute-start.12 = (f32[5,128,128]{2,1,0:T(8,128)S(1)}, f32[5,128,128]{2,1,0:T(8,128)S(1)}, u32[]{:S(2)}, u32[]{:S(2)}) collective-permute-start(f32[5,128,128]{2,1,0:T(8,128)S(1)} %get-tuple-element.27), channel_id=1, source_target_pairs={{0,16},{16,32},{32,48},{48,0},{64,80},{80,96},{96,112},{112,64},{1... | collective-permute-start | bytes 983048 | tf_op jit(solution)/shard_map/ppermute | solution.py:260
  120.0 10.7 %collective-permute-start.13 = (f32[5,128,128]{2,1,0:T(8,128)S(1)}, f32[5,128,128]{2,1,0:T(8,128)S(1)}, u32[]{:S(2)}, u32[]{:S(2)}) collective-permute-start(f32[5,128,128]{2,1,0:T(8,128)S(1)} %get-tuple-element.28), channel_id=1, source_target_pairs={{0,48},{16,0},{32,16},{48,32},{64,112},{80,64},{96,80},{112,96},{1... | collective-permute-start | bytes 983048 | tf_op jit(solution)/shard_map/ppermute | solution.py:260
